TPU v7x, 512 devices: a whole 4x8x8 slice. The times are simulated.
512 devices in a mesh: depth: 32 (over x_lo, y, core), height: 16 (over x_hi, z).
Axes of the slice: x: 4 (x_hi: 2, x_lo: 2; x = x_hi * 2 + x_lo), y: 8, z: 8, core: 2. Of those that a mesh axis runs over, the one named last changes fastest.
Arguments:
- volume: bfloat16 [4, 128, 128, 512], P(None, 'depth', 'height'), may hold values from -6 to 6
- first_kernel: bfloat16 [3, 3, 3, 4, 32], replicated, may hold values from -1.25 to 1.25
- second_kernel: bfloat16 [3, 3, 3, 32, 64], replicated, may hold values from -0.4375 to 0.4375
- third_kernel: bfloat16 [3, 3, 3, 64, 128], replicated, may hold values from -0.3125 to 0.3125
Outputs:
- features: bfloat16 [128, 32, 32, 128], P(None, 'depth', 'height')
All inputs are finite; a program needn't handle non-finite values.
Results may differ from a plain program's by a relative error of at most 0.013.
Values may be sent and summed in bfloat16 or wider, within the bound.
A program may use at most 64 MiB of HBM per device.

v0:
```python
import jax
import jax.numpy as jnp
from jax import lax
from jax.sharding import PartitionSpec as P

slope = 0.3


def with_halo(value, sides, width):
    for axis, dim in sides:
        peers, length = (lax.axis_size(axis), value.shape[dim])
        up = [(i, (i + 1) % peers) for i in range(peers - 1)]
        down = [(j, i) for i, j in up]
        last = lax.slice_in_dim(value, length - width, length, axis=dim)
        initial = lax.slice_in_dim(value, 0, width, axis=dim)
        before = lax.ppermute(last, axis, up)
        after = lax.ppermute(initial, axis, down)
        value = jnp.concatenate([before, value, after], axis=dim)
    return value


def leaky_relu(values):
    return jnp.where(values > 0, values, slope * values)


def pool_pairs(values):
    channels, deep_size, tall_size, wide_size = values.shape
    blocks = values.reshape(channels, deep_size // 2, 2, tall_size // 2, 2, wide_size)
    planes = jnp.max(blocks, axis=(2, 4))
    return jnp.maximum(planes[..., 0::2], planes[..., 1::2])


def width_taps(field):
    wide_size = field.shape[3]
    widened = jnp.pad(field, ((0, 0), (0, 0), (0, 0), (1, 1)))
    return jnp.stack([widened[..., tap_w : tap_w + wide_size] for tap_w in range(3)], 0)


def conv_sum(shifted, kernel, deep_size, tall_size):
    total = None
    for tap_d in range(3):
        for tap_h in range(3):
            window = shifted[:, :, tap_d : tap_d + deep_size, tap_h : tap_h + tall_size, :]
            term = jnp.einsum(
                "ecdhw,eco->odhw", window, kernel[tap_d, tap_h], preferred_element_type=jnp.float32
            )
            total = term if total is None else total + term
    return total


def faces(field):
    return with_halo(field, (("depth", 1), ("height", 2)), 1)


def conv_pool(field, kernel):
    channels, deep_size, tall_size, wide_size = field.shape
    shifted = width_taps(faces(field))
    result = conv_sum(shifted, kernel, deep_size, tall_size)
    return pool_pairs(leaky_relu(result)).astype(jnp.bfloat16)


def shards(volume, first_kernel, second_kernel, third_kernel):
    pooled_one = conv_pool(volume, first_kernel)
    pooled_two = conv_pool(pooled_one, second_kernel)
    channels, deep_size, tall_size, wide_size = pooled_two.shape
    outputs = third_kernel.shape[4]
    groups = lax.axis_size("height")
    slice_width = channels // groups
    beside_all = with_halo(pooled_two, (("depth", 1), ("height", 2)), 1)
    shifted = width_taps(beside_all)
    grouped = shifted.reshape(3, groups, slice_width, deep_size + 2, tall_size + 2, wide_size)
    partial_sums = None
    for tap_d in range(3):
        for tap_h in range(3):
            window = grouped[:, :, :, tap_d : tap_d + deep_size, tap_h : tap_h + tall_size, :]
            weights = third_kernel[tap_d, tap_h].reshape(3, groups, slice_width, outputs)
            term = jnp.einsum(
                "egsdhw,egso->godhw", window, weights, preferred_element_type=jnp.float32
            )
            partial_sums = term if partial_sums is None else partial_sums + term
    rounded = partial_sums.astype(jnp.bfloat16).astype(jnp.float32)
    total = jnp.sum(rounded, axis=0)
    return leaky_relu(total).astype(jnp.bfloat16)


def solution(mesh):
    in_specs = (P(None, "depth", "height", None), P(), P(), P())
    out_specs = P(None, "depth", "height", None)
    return jax.shard_map(shards, mesh=mesh, in_specs=in_specs, out_specs=out_specs, check_vma=False)
```

profile of v0, /device:TPU:6, one launch (start us, length us, event | category | flops | bytes accessed | tf_op | source)
XLA Modules:
  0.0 97.9 jit_solution(15951611043046248978)
XLA Ops:
  0.8 1.9 %collective-permute-start = (bf16[4,1,8,512]{3,0,2,1:T(4,128)(2,1)S(1)}, bf16[4,1,8,512]{3,0,2,1:T(4,128)(2,1)S(1)}, u32[]{:S(2)}, u32[]{:S(2)}) collective-permute-start(bf16[4,1,8,512]{3,0,2,1:T(4,128)(2,1)S(1)} %copy.170), channel_id=1, source_target_pairs={{0,16},{16,32},{32,48},{48,64},{64,80},{80,96},{96,112},{112,128},... | collective-permute-start | bytes 98312 | tf_op jit(solution)/shard_map/ppermute | solution.py:16
  2.8 5.8 %collective-permute-start.1 = (bf16[4,1,8,512]{3,0,2,1:T(4,128)(2,1)S(1)}, bf16[4,1,8,512]{3,0,2,1:T(4,128)(2,1)S(1)}, u32[]{:S(2)}, u32[]{:S(2)}) collective-permute-start(bf16[4,1,8,512]{3,0,2,1:T(4,128)(2,1)S(1)} %copy.171), channel_id=1, source_target_pairs={{16,0},{32,16},{48,32},{64,48},{80,64},{96,80},{112,96},{128,112},... | collective-permute-start | bytes 98312 | tf_op jit(solution)/shard_map/ppermute | solution.py:17
  8.6 1.0 %constant_dynamic-update-slice_fusion.1 = bf16[4,6,8,512]{3,0,2,1:T(4,128)(2,1)S(1)} fusion(bf16[4,6,8,512]{3,0,2,1:T(4,128)(2,1)S(1)} %constant_dynamic-update-slice_fusion.2, bf16[4,4,8,512]{3,2,1,0:T(8,128)(2,1)} %param.4), kind=kLoop, calls=%fused_computation.109 | loop fusion | bytes 262144
  10.1 4.3 %collective-permute-start.2 = (bf16[4,6,1,512]{3,0,2,1:T(4,128)(2,1)S(1)}, bf16[4,6,1,512]{3,0,2,1:T(4,128)(2,1)S(1)}, u32[]{:S(2)}, u32[]{:S(2)}) collective-permute-start(bf16[4,6,1,512]{3,0,2,1:T(4,128)(2,1)S(1)} %get-tuple-element.31), channel_id=1, source_target_pairs={{0,1},{1,2},{2,3},{3,4},{4,5},{5,6},{6,7},{7,8},{8,9},{9,10},{10,1... | collective-permute-start | bytes 73736 | tf_op jit(solution)/shard_map/ppermute | solution.py:16
  14.4 9.4 %collective-permute-start.3 = (bf16[4,6,1,512]{3,0,2,1:T(4,128)(2,1)S(1)}, bf16[4,6,1,512]{3,0,2,1:T(4,128)(2,1)S(1)}, u32[]{:S(2)}, u32[]{:S(2)}) collective-permute-start(bf16[4,6,1,512]{3,0,2,1:T(4,128)(2,1)S(1)} %get-tuple-element.32), channel_id=1, source_target_pairs={{1,0},{2,1},{3,2},{4,3},{5,4},{6,5},{7,6},{8,7},{9,8},{10,9},{11,1... | collective-permute-start | bytes 73736 | tf_op jit(solution)/shard_map/ppermute | solution.py:17
  23.9 1.5 %collective-permute-done.3 = bf16[4,6,1,512]{3,0,2,1:T(4,128)(2,1)S(1)} collective-permute-done((bf16[4,6,1,512]{3,0,2,1:T(4,128)(2,1)S(1)}, bf16[4,6,1,512]{3,0,2,1:T(4,128)(2,1)S(1)}, u32[]{:S(2)}, u32[]{:S(2)}) %collective-permute-start.3) | collective-permute-done | bytes 24608 | tf_op jit(solution)/shard_map/ppermute | solution.py:17
  31.0 2.6 %compare_select_fusion = bf16[32,4,8,512]{3,0,2,1:T(8,128)(2,1)S(1)} fusion(f32[4,8,512,32,1]{2,3,4,1,0:T(8,128)S(1)} %fusion.52, f32[4,8,512,32,1]{2,3,4,1,0:T(8,128)S(1)} %fusion.54, f32[4,8,512,32,1]{2,3,4,1,0:T(8,128)S(1)} %fusion.56, f32[4,8,512,32,1]{2,3,4,1,0:T(8,128)S(1)} %fusion.58, f32[4,8,512,32,1]{2,3,4,1,0:T(8,128)S(1)} %fusion.60, ...), kind=kOutput, calls=%fused_computation | convolution fusion | flops 20561920 | bytes 18566144 | tf_op jit(solution)/shard_map/ecdhw,eco->odhw/dot_general | solution.py:44
  33.8 4.5 %slice.249 = bf16[32,2,4,256]{3,0,2,1:T(8,128)(2,1)S(1)} slice(bf16[32,2,4,512]{3,0,2,1:T(8,128)(2,1)S(1)} %reduce_max.22), slice={[0:32:1], [0:2:1], [0:4:1], [0:512:2]} | slice | bytes 262144 | tf_op jit(solution)/shard_map/slice | solution.py:30
  38.3 4.5 %slice.250 = bf16[32,2,4,256]{3,0,2,1:T(8,128)(2,1)S(1)} slice(bf16[32,2,4,512]{3,0,2,1:T(8,128)(2,1)S(1)} %reduce_max.22), slice={[0:32:1], [0:2:1], [0:4:1], [1:512:2]} | slice | bytes 262144 | tf_op jit(solution)/shard_map/slice | solution.py:30
  42.9 1.9 %collective-permute-start.4 = (bf16[32,1,4,256]{3,0,2,1:T(8,128)(2,1)S(1)}, bf16[32,1,4,256]{3,0,2,1:T(8,128)(2,1)S(1)}, u32[]{:S(2)}, u32[]{:S(2)}) collective-permute-start(bf16[32,1,4,256]{3,0,2,1:T(8,128)(2,1)S(1)} %get-tuple-element.33), channel_id=1, source_target_pairs={{0,16},{16,32},{32,48},{48,64},{64,80},{80,96},{96,112},{112,128},... | collective-permute-start | bytes 196616 | tf_op jit(solution)/shard_map/ppermute | solution.py:16
  44.8 5.9 %collective-permute-start.5 = (bf16[32,1,4,256]{3,0,2,1:T(8,128)(2,1)S(1)}, bf16[32,1,4,256]{3,0,2,1:T(8,128)(2,1)S(1)}, u32[]{:S(2)}, u32[]{:S(2)}) collective-permute-start(bf16[32,1,4,256]{3,0,2,1:T(8,128)(2,1)S(1)} %get-tuple-element.34), channel_id=1, source_target_pairs={{16,0},{32,16},{48,32},{64,48},{80,64},{96,80},{112,96},{128,112},... | collective-permute-start | bytes 196616 | tf_op jit(solution)/shard_map/ppermute | solution.py:17
  50.8 1.7 %collective-permute-done.5 = bf16[32,1,4,256]{3,0,2,1:T(8,128)(2,1)S(1)} collective-permute-done((bf16[32,1,4,256]{3,0,2,1:T(8,128)(2,1)S(1)}, bf16[32,1,4,256]{3,0,2,1:T(8,128)(2,1)S(1)}, u32[]{:S(2)}, u32[]{:S(2)}) %collective-permute-start.5) | collective-permute-done | bytes 65568 | tf_op jit(solution)/shard_map/ppermute | solution.py:17
  52.5 1.9 %collective-permute-start.6 = (bf16[32,4,1,256]{3,0,2,1:T(8,128)(2,1)S(1)}, bf16[32,4,1,256]{3,0,2,1:T(8,128)(2,1)S(1)}, u32[]{:S(2)}, u32[]{:S(2)}) collective-permute-start(bf16[32,4,1,256]{3,0,2,1:T(8,128)(2,1)S(1)} %get-tuple-element.25), channel_id=1, source_target_pairs={{0,1},{1,2},{2,3},{3,4},{4,5},{5,6},{6,7},{7,8},{8,9},{9,10},{10,1... | collective-permute-start | bytes 196616 | tf_op jit(solution)/shard_map/ppermute | solution.py:16
  54.4 7.8 %collective-permute-start.7 = (bf16[32,4,1,256]{3,0,2,1:T(8,128)(2,1)S(1)}, bf16[32,4,1,256]{3,0,2,1:T(8,128)(2,1)S(1)}, u32[]{:S(2)}, u32[]{:S(2)}) collective-permute-start(bf16[32,4,1,256]{3,0,2,1:T(8,128)(2,1)S(1)} %get-tuple-element.26), channel_id=1, source_target_pairs={{1,0},{2,1},{3,2},{4,3},{5,4},{6,5},{7,6},{8,7},{9,8},{10,9},{11,1... | collective-permute-start | bytes 196616 | tf_op jit(solution)/shard_map/ppermute | solution.py:17
  62.5 1.6 %collective-permute-done.7 = bf16[32,4,1,256]{3,0,2,1:T(8,128)(2,1)S(1)} collective-permute-done((bf16[32,4,1,256]{3,0,2,1:T(8,128)(2,1)S(1)}, bf16[32,4,1,256]{3,0,2,1:T(8,128)(2,1)S(1)}, u32[]{:S(2)}, u32[]{:S(2)}) %collective-permute-start.7) | collective-permute-done | bytes 65568 | tf_op jit(solution)/shard_map/ppermute | solution.py:17
  67.3 1.2 %slice.275 = bf16[64,1,2,128]{3,0,2,1:T(8,128)(2,1)S(1)} slice(bf16[64,1,2,256]{3,0,2,1:T(8,128)(2,1)S(1)} %bitcast.376), slice={[0:64:1], [0:1:1], [0:2:1], [0:256:2]} | slice | bytes 65536 | tf_op jit(solution)/shard_map/slice | solution.py:30
  68.5 1.2 %slice.276 = bf16[64,1,2,128]{3,0,2,1:T(8,128)(2,1)S(1)} slice(bf16[64,1,2,256]{3,0,2,1:T(8,128)(2,1)S(1)} %bitcast.377), slice={[0:64:1], [0:1:1], [0:2:1], [1:256:2]} | slice | bytes 65536 | tf_op jit(solution)/shard_map/slice | solution.py:30
  69.7 1.9 %collective-permute-start.8 = (bf16[64,1,2,128]{3,0,2,1:T(8,128)(2,1)S(1)}, bf16[64,1,2,128]{3,0,2,1:T(8,128)(2,1)S(1)}, u32[]{:S(2)}, u32[]{:S(2)}) collective-permute-start(bf16[64,1,2,128]{3,0,2,1:T(8,128)(2,1)S(1)} %max.11), channel_id=1, source_target_pairs={{0,16},{16,32},{32,48},{48,64},{64,80},{80,96},{96,112},{112,128},... | collective-permute-start | bytes 98312 | tf_op jit(solution)/shard_map/ppermute | solution.py:16
  71.6 5.8 %collective-permute-start.9 = (bf16[64,1,2,128]{3,0,2,1:T(8,128)(2,1)S(1)}, bf16[64,1,2,128]{3,0,2,1:T(8,128)(2,1)S(1)}, u32[]{:S(2)}, u32[]{:S(2)}) collective-permute-start(bf16[64,1,2,128]{3,0,2,1:T(8,128)(2,1)S(1)} %max.11), channel_id=1, source_target_pairs={{16,0},{32,16},{48,32},{64,48},{80,64},{96,80},{112,96},{128,112},... | collective-permute-start | bytes 98312 | tf_op jit(solution)/shard_map/ppermute | solution.py:17
  77.4 1.6 %collective-permute-done.9 = bf16[64,1,2,128]{3,0,2,1:T(8,128)(2,1)S(1)} collective-permute-done((bf16[64,1,2,128]{3,0,2,1:T(8,128)(2,1)S(1)}, bf16[64,1,2,128]{3,0,2,1:T(8,128)(2,1)S(1)}, u32[]{:S(2)}, u32[]{:S(2)}) %collective-permute-start.9) | collective-permute-done | bytes 32800 | tf_op jit(solution)/shard_map/ppermute | solution.py:17
  79.0 1.9 %collective-permute-start.10 = (bf16[64,3,1,128]{3,0,2,1:T(8,128)(2,1)S(1)}, bf16[64,3,1,128]{3,0,2,1:T(8,128)(2,1)S(1)}, u32[]{:S(2)}, u32[]{:S(2)}) collective-permute-start(bf16[64,3,1,128]{3,0,2,1:T(8,128)(2,1)S(1)} %get-tuple-element.37), channel_id=1, source_target_pairs={{0,1},{1,2},{2,3},{3,4},{4,5},{5,6},{6,7},{7,8},{8,9},{9,10},{10,1... | collective-permute-start | bytes 147464 | tf_op jit(solution)/shard_map/ppermute | solution.py:16
  80.9 7.9 %collective-permute-start.11 = (bf16[64,3,1,128]{3,0,2,1:T(8,128)(2,1)S(1)}, bf16[64,3,1,128]{3,0,2,1:T(8,128)(2,1)S(1)}, u32[]{:S(2)}, u32[]{:S(2)}) collective-permute-start(bf16[64,3,1,128]{3,0,2,1:T(8,128)(2,1)S(1)} %get-tuple-element.38), channel_id=1, source_target_pairs={{1,0},{2,1},{3,2},{4,3},{5,4},{6,5},{7,6},{8,7},{9,8},{10,9},{11,1... | collective-permute-start | bytes 147464 | tf_op jit(solution)/shard_map/ppermute | solution.py:17
  88.9 1.6 %collective-permute-done.11 = bf16[64,3,1,128]{3,0,2,1:T(8,128)(2,1)S(1)} collective-permute-done((bf16[64,3,1,128]{3,0,2,1:T(8,128)(2,1)S(1)}, bf16[64,3,1,128]{3,0,2,1:T(8,128)(2,1)S(1)}, u32[]{:S(2)}, u32[]{:S(2)}) %collective-permute-start.11) | collective-permute-done | bytes 49184 | tf_op jit(solution)/shard_map/ppermute | solution.py:17
  95.8 1.3 %convert_reduce_fusion = f32[2,128,128]{2,1,0:T(8,128)S(1)} fusion(f32[16,2,128,128,1]{3,2,4,1,0:T(8,128)S(1)} %fusion.16, f32[16,2,128,128,1]{3,2,4,1,0:T(8,128)S(1)} %fusion.17, f32[16,2,128,128,1]{3,2,4,1,0:T(8,128)S(1)} %fusion.18, f32[16,2,128,128,1]{3,2,4,1,0:T(8,128)S(1)} %fusion.19, f32[16,2,128,128,1]{3,2,4,1,0:T(8,128)S(1)} %fusion.20, ...), kind=kOutput, calls=%fused_computation.18 | convolution fusion | flops 18317312 | bytes 17055744 | tf_op jit(solution)/shard_map/egsdhw,egso->godhw/dot_general | solution.py:77
  (65 shorter events, 16.8 us)
Async XLA Ops:
  0.0 26.1 %copy-start.1 = (bf16[3,3,3,4,32]{4,3,2,1,0:T(4,128)(2,1)S(1)}, bf16[3,3,3,4,32]{4,3,2,1,0:T(4,128)(2,1)}, u32[]{:S(2)}) copy-start(bf16[3,3,3,4,32]{4,3,2,1,0:T(4,128)(2,1)} %param.5) | copy-start | bytes 20740
  0.8 7.7 %collective-permute-start = (bf16[4,1,8,512]{3,0,2,1:T(4,128)(2,1)S(1)}, bf16[4,1,8,512]{3,0,2,1:T(4,128)(2,1)S(1)}, u32[]{:S(2)}, u32[]{:S(2)}) collective-permute-start(bf16[4,1,8,512]{3,0,2,1:T(4,128)(2,1)S(1)} %copy.170), channel_id=1, source_target_pairs={{0,16},{16,32},{32,48},{48,64},{64,80},{80,96},{96,112},{112,128},... | collective-permute-start | bytes 98312 | tf_op jit(solution)/shard_map/ppermute | solution.py:16
  2.8 7.3 %collective-permute-start.1 = (bf16[4,1,8,512]{3,0,2,1:T(4,128)(2,1)S(1)}, bf16[4,1,8,512]{3,0,2,1:T(4,128)(2,1)S(1)}, u32[]{:S(2)}, u32[]{:S(2)}) collective-permute-start(bf16[4,1,8,512]{3,0,2,1:T(4,128)(2,1)S(1)} %copy.171), channel_id=1, source_target_pairs={{16,0},{32,16},{48,32},{64,48},{80,64},{96,80},{112,96},{128,112},... | collective-permute-start | bytes 98312 | tf_op jit(solution)/shard_map/ppermute | solution.py:17
  10.1 13.7 %collective-permute-start.2 = (bf16[4,6,1,512]{3,0,2,1:T(4,128)(2,1)S(1)}, bf16[4,6,1,512]{3,0,2,1:T(4,128)(2,1)S(1)}, u32[]{:S(2)}, u32[]{:S(2)}) collective-permute-start(bf16[4,6,1,512]{3,0,2,1:T(4,128)(2,1)S(1)} %get-tuple-element.31), channel_id=1, source_target_pairs={{0,1},{1,2},{2,3},{3,4},{4,5},{5,6},{6,7},{7,8},{8,9},{9,10},{10,1... | collective-permute-start | bytes 73736 | tf_op jit(solution)/shard_map/ppermute | solution.py:16
  14.4 10.9 %collective-permute-start.3 = (bf16[4,6,1,512]{3,0,2,1:T(4,128)(2,1)S(1)}, bf16[4,6,1,512]{3,0,2,1:T(4,128)(2,1)S(1)}, u32[]{:S(2)}, u32[]{:S(2)}) collective-permute-start(bf16[4,6,1,512]{3,0,2,1:T(4,128)(2,1)S(1)} %get-tuple-element.32), channel_id=1, source_target_pairs={{1,0},{2,1},{3,2},{4,3},{5,4},{6,5},{7,6},{8,7},{9,8},{10,9},{11,1... | collective-permute-start | bytes 73736 | tf_op jit(solution)/shard_map/ppermute | solution.py:17
  38.3 26.3 %copy-start.2 = (bf16[3,3,3,32,64]{4,3,2,1,0:T(8,128)(2,1)S(1)}, bf16[3,3,3,32,64]{4,3,2,1,0:T(8,128)(2,1)}, u32[]{:S(2)}) copy-start(bf16[3,3,3,32,64]{4,3,2,1,0:T(8,128)(2,1)} %param.6) | copy-start | bytes 331780
  42.9 7.9 %collective-permute-start.4 = (bf16[32,1,4,256]{3,0,2,1:T(8,128)(2,1)S(1)}, bf16[32,1,4,256]{3,0,2,1:T(8,128)(2,1)S(1)}, u32[]{:S(2)}, u32[]{:S(2)}) collective-permute-start(bf16[32,1,4,256]{3,0,2,1:T(8,128)(2,1)S(1)} %get-tuple-element.33), channel_id=1, source_target_pairs={{0,16},{16,32},{32,48},{48,64},{64,80},{80,96},{96,112},{112,128},... | collective-permute-start | bytes 196616 | tf_op jit(solution)/shard_map/ppermute | solution.py:16
  44.8 7.6 %collective-permute-start.5 = (bf16[32,1,4,256]{3,0,2,1:T(8,128)(2,1)S(1)}, bf16[32,1,4,256]{3,0,2,1:T(8,128)(2,1)S(1)}, u32[]{:S(2)}, u32[]{:S(2)}) collective-permute-start(bf16[32,1,4,256]{3,0,2,1:T(8,128)(2,1)S(1)} %get-tuple-element.34), channel_id=1, source_target_pairs={{16,0},{32,16},{48,32},{64,48},{80,64},{96,80},{112,96},{128,112},... | collective-permute-start | bytes 196616 | tf_op jit(solution)/shard_map/ppermute | solution.py:17
  52.5 10.1 %collective-permute-start.6 = (bf16[32,4,1,256]{3,0,2,1:T(8,128)(2,1)S(1)}, bf16[32,4,1,256]{3,0,2,1:T(8,128)(2,1)S(1)}, u32[]{:S(2)}, u32[]{:S(2)}) collective-permute-start(bf16[32,4,1,256]{3,0,2,1:T(8,128)(2,1)S(1)} %get-tuple-element.25), channel_id=1, source_target_pairs={{0,1},{1,2},{2,3},{3,4},{4,5},{5,6},{6,7},{7,8},{8,9},{9,10},{10,1... | collective-permute-start | bytes 196616 | tf_op jit(solution)/shard_map/ppermute | solution.py:16
  54.4 9.7 %collective-permute-start.7 = (bf16[32,4,1,256]{3,0,2,1:T(8,128)(2,1)S(1)}, bf16[32,4,1,256]{3,0,2,1:T(8,128)(2,1)S(1)}, u32[]{:S(2)}, u32[]{:S(2)}) collective-permute-start(bf16[32,4,1,256]{3,0,2,1:T(8,128)(2,1)S(1)} %get-tuple-element.26), channel_id=1, source_target_pairs={{1,0},{2,1},{3,2},{4,3},{5,4},{6,5},{7,6},{8,7},{9,8},{10,9},{11,1... | collective-permute-start | bytes 196616 | tf_op jit(solution)/shard_map/ppermute | solution.py:17
  66.8 22.0 %copy-start = (bf16[3,3,3,64,128]{4,3,2,1,0:T(8,128)(2,1)S(1)}, bf16[3,3,3,64,128]{4,3,2,1,0:T(8,128)(2,1)}, u32[]{:S(2)}) copy-start(bf16[3,3,3,64,128]{4,3,2,1,0:T(8,128)(2,1)} %param.7) | copy-start | bytes 1327108
  69.7 7.7 %collective-permute-start.8 = (bf16[64,1,2,128]{3,0,2,1:T(8,128)(2,1)S(1)}, bf16[64,1,2,128]{3,0,2,1:T(8,128)(2,1)S(1)}, u32[]{:S(2)}, u32[]{:S(2)}) collective-permute-start(bf16[64,1,2,128]{3,0,2,1:T(8,128)(2,1)S(1)} %max.11), channel_id=1, source_target_pairs={{0,16},{16,32},{32,48},{48,64},{64,80},{80,96},{96,112},{112,128},... | collective-permute-start | bytes 98312 | tf_op jit(solution)/shard_map/ppermute | solution.py:16
  71.6 7.3 %collective-permute-start.9 = (bf16[64,1,2,128]{3,0,2,1:T(8,128)(2,1)S(1)}, bf16[64,1,2,128]{3,0,2,1:T(8,128)(2,1)S(1)}, u32[]{:S(2)}, u32[]{:S(2)}) collective-permute-start(bf16[64,1,2,128]{3,0,2,1:T(8,128)(2,1)S(1)} %max.11), channel_id=1, source_target_pairs={{16,0},{32,16},{48,32},{64,48},{80,64},{96,80},{112,96},{128,112},... | collective-permute-start | bytes 98312 | tf_op jit(solution)/shard_map/ppermute | solution.py:17
  79.0 9.9 %collective-permute-start.10 = (bf16[64,3,1,128]{3,0,2,1:T(8,128)(2,1)S(1)}, bf16[64,3,1,128]{3,0,2,1:T(8,128)(2,1)S(1)}, u32[]{:S(2)}, u32[]{:S(2)}) collective-permute-start(bf16[64,3,1,128]{3,0,2,1:T(8,128)(2,1)S(1)} %get-tuple-element.37), channel_id=1, source_target_pairs={{0,1},{1,2},{2,3},{3,4},{4,5},{5,6},{6,7},{7,8},{8,9},{9,10},{10,1... | collective-permute-start | bytes 147464 | tf_op jit(solution)/shard_map/ppermute | solution.py:16
  80.9 9.6 %collective-permute-start.11 = (bf16[64,3,1,128]{3,0,2,1:T(8,128)(2,1)S(1)}, bf16[64,3,1,128]{3,0,2,1:T(8,128)(2,1)S(1)}, u32[]{:S(2)}, u32[]{:S(2)}) collective-permute-start(bf16[64,3,1,128]{3,0,2,1:T(8,128)(2,1)S(1)} %get-tuple-element.38), channel_id=1, source_target_pairs={{1,0},{2,1},{3,2},{4,3},{5,4},{6,5},{7,6},{8,7},{9,8},{10,9},{11,1... | collective-permute-start | bytes 147464 | tf_op jit(solution)/shard_map/ppermute | solution.py:17
where the time goes:
time: 98.4 us; the launch traced here: 97.9 us
  starting transfers between devices  56.5 us (57%)
  matrix products  15.5 us (16%)
  local copies, waits for them, and re-layouts  15.4 us (16%)
  waiting for transfers between devices  8.84 us (9%)
  other arithmetic  1.28 us (1%)
    ppermute x6, starting transfers between devices, with_halo(): after = lax.ppermute(initial, axis, down)  42.6 us
    ppermute x6, starting transfers between devices, with_halo(): before = lax.ppermute(last, axis, up)  13.9 us
    slice x4, local copies, waits for them, and re-layouts, pool_pairs(): return jnp.maximum(planes[..., 0::2], planes[..., 1::2])  11.3 us
    dot_general x18, matrix products, conv_sum(): jnp.einsum('ecdhw,eco->odhw', window, kernel[tap_d, tap_h], preferred_ele...  10.1 us
    ppermute x6, waiting for transfers between devices, with_halo(): after = lax.ppermute(initial, axis, down)  8.45 us
    dot_general x9, matrix products, shards(): jnp.einsum('egsdhw,egso->godhw', window, weights, preferred_element_type=...  5.4 us
  transfers between devices with their start and end apart: 12, of which 8 were waited for; matrix products, arithmetic and copies ran while one was open for 1% of the time, Pallas kernels for 0%

commit v1 on v0

v1 whole, which is shorter than its diff:
```python
import functools

import jax
import jax.numpy as jnp
import numpy as np
from jax import lax
from jax.experimental import pallas as pl
from jax.experimental.pallas import tpu as pltpu
from jax.sharding import PartitionSpec as P

MESH = pl.DeviceIdType.MESH
BF16 = jnp.bfloat16
F32 = jnp.float32
SLOPE = 0.3
SIDES = [(a, b) for a in (-1, 0, 1) for b in (-1, 0, 1) if (a, b) != (0, 0)]


def phase_matrix():
    matrix = np.zeros((512, 4, 128), np.float32)
    for t in range(4):
        for l in range(128):
            matrix[4 * l + t, t, l] = 1
    return matrix.reshape(512, 512)


def first_placement():
    place = np.zeros((3, 3, 3, 4, 2, 2, 2, 2, 4, 4, 4, 4), np.float32)
    order = ((1, 2, 3, 0), (3, 0, 1, 2))
    for a, b, e, c, s, pd, ph, pw in np.ndindex(3, 3, 3, 4, 2, 2, 2, 2):
        place[a, b, e, c, s, pd, ph, pw, pd + a, ph + b, order[s].index(pw + e), c] = 1
    return np.pad(place.reshape(108, 4096), ((0, 20), (0, 0)))


def nt_dot(left, right):
    return lax.dot_general(left, right, (((1,), (1,)), ((), ())), preferred_element_type=F32)


def dot(left, right):
    return jnp.dot(left, right, preferred_element_type=F32)


def eye(size):
    rows = lax.broadcasted_iota(jnp.int32, (size, size), 0)
    columns = lax.broadcasted_iota(jnp.int32, (size, size), 1)
    return jnp.where(rows == columns, 1.0, 0.0).astype(BF16)


def before(value):
    lane = lax.broadcasted_iota(jnp.int32, value.shape, 1)
    return jnp.where(lane == 0, 0.0, pltpu.roll(value, 1, 1))


def after(value):
    lane = lax.broadcasted_iota(jnp.int32, value.shape, 1)
    return jnp.where(lane == 127, 0.0, pltpu.roll(value, 127, 1))


def leaky(value):
    return jnp.where(value > 0, value, SLOPE * value)


def span(shift, size, halo, received):
    if shift == 0:
        return pl.ds(halo, size)
    if received:
        return pl.ds(0, halo) if shift == 1 else pl.ds(halo + size, halo)
    return pl.ds(size, halo) if shift == 1 else pl.ds(halo, halo)


def body(
    depths, heights,
    volume, first, second, third, phases, placement, out,
    x, k1, k2, k3, phase, place, y, g, e0, e1, k1f, w1, f, w2, t, u, w3, of, ob,
    load_sem, send_sem, recv_sem,
):
    di, hi = lax.axis_index("depth"), lax.axis_index("height")

    def within(a, b):
        return (di + a >= 0) & (di + a < depths) & (hi + b >= 0) & (hi + b < heights)

    loads = [
        pltpu.make_async_copy(source, target, load_sem.at[i])
        for i, (source, target) in enumerate(
            ((volume, x), (phases, phase), (first, k1), (placement, place), (second, k2), (third, k3))
        )
    ]
    for load in loads:
        load.start()

    barrier = pltpu.get_barrier_semaphore()
    for a, b in SIDES:
        @pl.when(within(a, b))
        def _():
            pl.semaphore_signal(barrier, inc=1, device_id=(di + a, hi + b), device_id_type=MESH)

    for a, b in SIDES:
        @pl.when(jnp.logical_not(within(-a, -b)))
        def _():
            d1, h1 = span(a, 4, 3, True), span(b, 8, 3, True)
            g[d1, h1] = jnp.zeros((d1.size, h1.size, 16, 128), BF16)
            d2, h2 = span(a, 1, 1, True), span(b, 2, 1, True)
            t[d2, h2] = jnp.zeros((d2.size, h2.size, 64, 128), BF16)

    loads[0].wait()
    loads[1].wait()
    spread = dot(x[...].reshape(128, 512), phase[...])
    for i in range(4):
        y[pl.ds(i * 128, 128), :] = spread[:, i * 128 : (i + 1) * 128]
    for d in range(4):
        for h in range(8):
            g[3 + d, 3 + h] = y[pl.ds(d * 8 + h, 16, stride=32), :].astype(BF16)

    count_d = 1 + (di > 0).astype(jnp.int32) + (di < depths - 1).astype(jnp.int32)
    count_h = 1 + (hi > 0).astype(jnp.int32) + (hi < heights - 1).astype(jnp.int32)
    pl.semaphore_wait(barrier, count_d * count_h - 1)

    def exchange(buffer, depth_size, height_size, halo, base):
        for i, (a, b) in enumerate(SIDES):
            copy = pltpu.make_async_remote_copy(
                src_ref=buffer.at[span(a, depth_size, halo, False), span(b, height_size, halo, False)],
                dst_ref=buffer.at[span(a, depth_size, halo, True), span(b, height_size, halo, True)],
                send_sem=send_sem.at[base + i],
                recv_sem=recv_sem.at[base + i],
                device_id=(di + a, hi + b),
                device_id_type=MESH,
            )
            yield (a, b), copy

    def start(buffer, depth_size, height_size, halo, base):
        for (a, b), copy in exchange(buffer, depth_size, height_size, halo, base):
            pl.when(within(a, b))(copy.start)

    def arrive(buffer, depth_size, height_size, halo, base):
        for (a, b), copy in exchange(buffer, depth_size, height_size, halo, base):
            pl.when(within(-a, -b))(copy.wait_recv)

    def sent(buffer, depth_size, height_size, halo, base):
        for (a, b), copy in exchange(buffer, depth_size, height_size, halo, base):
            pl.when(within(a, b))(copy.wait_send)

    start(g, 4, 8, 3, 0)

    for load in loads[2:]:
        load.wait()
    k1f[...] = jnp.zeros_like(k1f)
    for i, (a, b, e) in enumerate(np.ndindex(3, 3, 3)):
        k1f[pl.ds(4 * i, 4), :] = k1[a, b, e].astype(F32)
    flat = nt_dot(eye(32), k1f[...].astype(BF16)).astype(BF16)
    for s in range(2):
        for p in range(0, 8, 4):
            wide = dot(flat, place[:, pl.ds((s * 8 + p) * 256, 1024)]).astype(BF16)
            for q in range(4):
                w1[s, pl.ds((p + q) * 32, 32), :] = wide[:, q * 256 : (q + 1) * 256]

    unit = eye(64)
    blank = jnp.zeros((32, 64), BF16)
    for a in range(3):
        for b in range(3):
            taps = k2[a, b].reshape(96, 64)
            turned = nt_dot(unit, jnp.concatenate([taps, blank, blank, taps], 0)).astype(BF16)
            for ph in range(2):
                for pw in range(2):
                    w2[pl.ds(ph * 128 + pw * 64, 64), pl.ds((a * 4 + b + ph) * 128, 128)] = turned[
                        :, pw * 128 : (pw + 1) * 128
                    ]
        for ph, h in ((0, 3), (1, 0)):
            w2[pl.ds(ph * 128, 128), pl.ds((a * 4 + h) * 128, 128)] = jnp.zeros((128, 128), BF16)

    unit = eye(128)
    for i in range(9):
        rows = k3[i // 3, i % 3].reshape(192, 128)
        w3[i] = nt_dot(unit, rows).astype(BF16)

    arrive(g, 4, 8, 3, 0)

    @pl.loop(0, 10)
    def _(d):
        value = g[d].astype(F32)
        low, high = value[:, 0:8].reshape(112, 128), value[:, 8:16].reshape(112, 128)
        row = lax.broadcasted_iota(jnp.int32, (112, 128), 0) & 7
        turned = jnp.where(row >= 4, before(high), high)
        e0[d] = jnp.concatenate([value[:, 0:8], turned.reshape(14, 8, 128)], 1).astype(BF16)
        turned = jnp.where(row < 4, after(low), low)
        e1[d] = jnp.concatenate([turned.reshape(14, 8, 128), value[:, 8:16]], 1).astype(BF16)

    @pl.loop(0, 4)
    def _(dp):
        deep = 2 * di + dp - 1
        deep_in = (deep >= 0) & (deep < 2 * depths)
        for hp in range(0, 6, 2):
            halves = []
            for s, e in enumerate((e0, e1)):
                parts = [
                    e[pl.ds(2 * dp, 4), pl.ds(2 * (hp + j), 4)].reshape(256, 128) for j in range(2)
                ]
                sums = dot(w1[s], jnp.concatenate(parts, 1))
                halves.append(leaky(jnp.max(sums.reshape(8, 32, 256), axis=0)))
            for j in range(2):
                tall = 4 * hi + hp + j - 1
                keep = jnp.where(deep_in & (tall >= 0) & (tall < 4 * heights), 1.0, 0.0)
                p0, p1 = (half[:, j * 128 : (j + 1) * 128] * keep for half in halves)
                for i, part in enumerate((before(p1), p0, p1, after(p0))):
                    f[dp, hp + j, pl.ds(32 * i, 32), :] = part.astype(BF16)

    best = None
    for pd in range(2):
        parts = [f[pl.ds(pd, 3), pl.ds(2 * j, 4)].reshape(1536, 128) for j in range(2)]
        sums = dot(w2[...], jnp.concatenate(parts, 1))
        sums = jnp.max(sums.reshape(4, 64, 256), axis=0)
        best = sums if best is None else jnp.maximum(best, sums)
    best = leaky(best).astype(BF16)
    t[1, 1] = best[:, 0:128]
    t[1, 2] = best[:, 128:256]
    start(t, 1, 2, 1, 8)
    arrive(t, 1, 2, 1, 8)

    for d in range(3):
        for h in range(4):
            value = t[d, h].astype(F32)
            u[d, h, pl.ds(0, 64), :] = before(value).astype(BF16)
            u[d, h, pl.ds(64, 64), :] = t[d, h]
            u[d, h, pl.ds(128, 64), :] = after(value).astype(BF16)
    total = None
    for i in range(9):
        parts = [u[i // 3, i % 3 + j] for j in range(2)]
        term = dot(w3[i], jnp.concatenate(parts, 1))
        total = term if total is None else total + term
    total = leaky(total)
    of[pl.ds(0, 128, stride=2), :] = total[:, 0:128]
    of[pl.ds(1, 128, stride=2), :] = total[:, 128:256]
    ob[...] = of[...].astype(BF16)
    store = pltpu.make_async_copy(ob, out, load_sem.at[0])
    store.start()
    sent(g, 4, 8, 3, 0)
    sent(t, 1, 2, 1, 8)
    store.wait()


def shards(depths, heights, volume, first, second, third):
    phases = jnp.asarray(phase_matrix(), BF16)
    placement = jnp.asarray(first_placement(), BF16)
    result = pl.pallas_call(
        functools.partial(body, depths, heights),
        out_shape=jax.ShapeDtypeStruct((256, 128), BF16),
        in_specs=[pl.BlockSpec(memory_space=pl.ANY)] * 6,
        out_specs=pl.BlockSpec(memory_space=pl.ANY),
        scratch_shapes=[
            pltpu.VMEM((4, 4, 8, 512), BF16),
            pltpu.VMEM((3, 3, 3, 4, 32), BF16),
            pltpu.VMEM((3, 3, 96, 64), BF16),
            pltpu.VMEM((3, 3, 192, 128), BF16),
            pltpu.VMEM((512, 512), BF16),
            pltpu.VMEM((128, 4096), BF16),
            pltpu.VMEM((512, 128), F32),
            pltpu.VMEM((10, 14, 16, 128), BF16),
            pltpu.VMEM((10, 14, 16, 128), BF16),
            pltpu.VMEM((10, 14, 16, 128), BF16),
            pltpu.VMEM((128, 32), F32),
            pltpu.VMEM((2, 256, 256), BF16),
            pltpu.VMEM((4, 6, 128, 128), BF16),
            pltpu.VMEM((256, 1536), BF16),
            pltpu.VMEM((3, 4, 64, 128), BF16),
            pltpu.VMEM((3, 4, 192, 128), BF16),
            pltpu.VMEM((9, 128, 192), BF16),
            pltpu.VMEM((256, 128), F32),
            pltpu.VMEM((256, 128), BF16),
            pltpu.SemaphoreType.DMA((6,)),
            pltpu.SemaphoreType.DMA((16,)),
            pltpu.SemaphoreType.DMA((16,)),
        ],
        compiler_params=pltpu.CompilerParams(
            collective_id=0, has_side_effects=True, vmem_limit_bytes=48 * 2**20
        ),
        cost_estimate=pl.CostEstimate(flops=2 * 10**9, bytes_accessed=3 * 10**6, transcendentals=0),
        name="layers",
    )(volume, first, second.reshape(3, 3, 96, 64), third.reshape(3, 3, 192, 128), phases, placement)
    return result.reshape(128, 1, 2, 128)


def solution(mesh):
    in_specs = (P(None, "depth", "height", None), P(), P(), P())
    out_specs = P(None, "depth", "height", None)
    local = functools.partial(shards, mesh.shape["depth"], mesh.shape["height"])
    return jax.shard_map(local, mesh=mesh, in_specs=in_specs, out_specs=out_specs, check_vma=False)
```

time: 98.4 us -> 36.3 us (0.37)
  the two profiles are of different devices: /device:TPU:6 before, /device:TPU:31 now
where the time goes in v1:
time: 36.3 us; the launch traced here: 36 us
  Pallas kernels  29.5 us (81%)
  local copies, waits for them, and re-layouts  6.49 us (18%)
    pallas_call x1, Pallas kernels, shards(): pl.pallas_call(functools.partial(body, depths, heights), out_shape=jax.Sh...  29.5 us
    unnamed x13, local copies, waits for them, and re-layouts  6.49 us

profile of v1, /device:TPU:31, one launch (start us, length us, event | category | flops | bytes accessed | tf_op | source)
XLA Modules:
  0.0 36.0 jit_solution(2401927521497767613)
XLA Ops:
  0.0 0.0 copy-start
  0.0 1.0 %copy-done = bf16[3,3,3,64,128]{4,3,2,1,0:T(8,128)(2,1)S(1)} copy-done((bf16[3,3,3,64,128]{4,3,2,1,0:T(8,128)(2,1)S(1)}, bf16[3,3,3,64,128]{4,3,2,1,0:T(8,128)(2,1)}, u32[]{:S(2)}) %copy-start) | copy-done | bytes 442392
  1.0 0.0 copy-start.1
  1.0 0.9 %copy-done.1 = bf16[3,3,3,32,64]{4,3,2,1,0:T(8,128)(2,1)S(1)} copy-done((bf16[3,3,3,32,64]{4,3,2,1,0:T(8,128)(2,1)S(1)}, bf16[3,3,3,32,64]{4,3,2,1,0:T(8,128)(2,1)}, u32[]{:S(2)}) %copy-start.1) | copy-done | bytes 110616
  2.0 0.0 copy-start.2
  2.0 0.9 %copy-done.2 = bf16[4,4,8,512]{3,2,1,0:T(8,128)(2,1)S(1)} copy-done((bf16[4,4,8,512]{3,2,1,0:T(8,128)(2,1)S(1)}, bf16[4,4,8,512]{3,2,1,0:T(8,128)(2,1)}, u32[]{:S(2)}) %copy-start.2) | copy-done | bytes 131096
  2.9 0.0 copy-start.3
  2.9 0.7 %copy-done.3 = bf16[3,3,3,4,32]{4,3,2,1,0:T(4,128)(2,1)S(1)} copy-done((bf16[3,3,3,4,32]{4,3,2,1,0:T(4,128)(2,1)S(1)}, bf16[3,3,3,4,32]{4,3,2,1,0:T(4,128)(2,1)}, u32[]{:S(2)}) %copy-start.3) | copy-done | bytes 6936
  3.6 0.0 copy-start.4
  3.6 1.2 %copy-done.4 = bf16[128,4096]{1,0:T(8,128)(2,1)S(1)} copy-done((bf16[128,4096]{1,0:T(8,128)(2,1)S(1)}, bf16[128,4096]{1,0:T(8,128)(2,1)}, u32[]{:S(2)}) %copy-start.4) | copy-done | bytes 1048600
  4.8 0.0 copy-start.5
  4.8 1.0 %copy-done.5 = bf16[512,512]{1,0:T(8,128)(2,1)S(1)} copy-done((bf16[512,512]{1,0:T(8,128)(2,1)S(1)}, bf16[512,512]{1,0:T(8,128)(2,1)}, u32[]{:S(2)}) %copy-start.5) | copy-done | bytes 524312
  5.9 29.5 %layers.1 = bf16[256,128]{1,0:T(8,128)(2,1)S(1)} custom-call(bf16[4,4,8,512]{3,2,1,0:T(8,128)(2,1)S(1)} %copy-done.2, bf16[3,3,3,4,32]{4,3,2,1,0:T(4,128)(2,1)S(1)} %copy-done.3, bf16[3,3,96,64]{3,2,1,0:T(8,128)(2,1)S(1)} %bitcast.7, bf16[3,3,192,128]{3,2,1,0:T(8,128)(2,1)S(1)} %bitcast.6, bf16[512,512]{1,0:T(8,128)(2,1)S(1)} %copy-done.5, ...), custom_call_target="tpu_custom_call" | custom-call | flops 2000000000 | bytes 3000000 | tf_op jit(solution)/shard_map/layers/pallas_call | solution.py:242
  35.4 0.6 %copy.9 = bf16[128,1,2,128]{3,2,1,0:T(2,128)(2,1)} copy(bf16[128,1,2,128]{3,2,1,0:T(2,128)(2,1)S(1)} %bitcast.5) | data formatting | bytes 131072
Async XLA Ops:
  0.0 1.0 %copy-start = (bf16[3,3,3,64,128]{4,3,2,1,0:T(8,128)(2,1)S(1)}, bf16[3,3,3,64,128]{4,3,2,1,0:T(8,128)(2,1)}, u32[]{:S(2)}) copy-start(bf16[3,3,3,64,128]{4,3,2,1,0:T(8,128)(2,1)} %param.9) | copy-start | bytes 1327108
  1.0 0.9 %copy-start.1 = (bf16[3,3,3,32,64]{4,3,2,1,0:T(8,128)(2,1)S(1)}, bf16[3,3,3,32,64]{4,3,2,1,0:T(8,128)(2,1)}, u32[]{:S(2)}) copy-start(bf16[3,3,3,32,64]{4,3,2,1,0:T(8,128)(2,1)} %param.8) | copy-start | bytes 331780
  2.0 0.9 %copy-start.2 = (bf16[4,4,8,512]{3,2,1,0:T(8,128)(2,1)S(1)}, bf16[4,4,8,512]{3,2,1,0:T(8,128)(2,1)}, u32[]{:S(2)}) copy-start(bf16[4,4,8,512]{3,2,1,0:T(8,128)(2,1)} %volume.1) | copy-start | bytes 393220
  2.9 0.7 %copy-start.3 = (bf16[3,3,3,4,32]{4,3,2,1,0:T(4,128)(2,1)S(1)}, bf16[3,3,3,4,32]{4,3,2,1,0:T(4,128)(2,1)}, u32[]{:S(2)}) copy-start(bf16[3,3,3,4,32]{4,3,2,1,0:T(4,128)(2,1)} %first.1) | copy-start | bytes 20740
  3.6 1.2 %copy-start.4 = (bf16[128,4096]{1,0:T(8,128)(2,1)S(1)}, bf16[128,4096]{1,0:T(8,128)(2,1)}, u32[]{:S(2)}) copy-start(bf16[128,4096]{1,0:T(8,128)(2,1)} %constant.5.clone.placement) | copy-start | bytes 3145732
  4.8 1.0 %copy-start.5 = (bf16[512,512]{1,0:T(8,128)(2,1)S(1)}, bf16[512,512]{1,0:T(8,128)(2,1)}, u32[]{:S(2)}) copy-start(bf16[512,512]{1,0:T(8,128)(2,1)} %constant.4.clone.phases) | copy-start | bytes 1572868

commit v2 on v1

--- a/solution.py
+++ b/solution.py
@@ -241,9 +241,9 @@
     placement = jnp.asarray(first_placement(), BF16)
     result = pl.pallas_call(
         functools.partial(body, depths, heights),
-        out_shape=jax.ShapeDtypeStruct((256, 128), BF16),
-        in_specs=[pl.BlockSpec(memory_space=pl.ANY)] * 6,
-        out_specs=pl.BlockSpec(memory_space=pl.ANY),
+        out_shape=pltpu.VMEM((256, 128), BF16),
+        in_specs=[pl.BlockSpec(memory_space=pltpu.HBM)] * 6,
+        out_specs=pl.BlockSpec(memory_space=pltpu.VMEM),
         scratch_shapes=[
             pltpu.VMEM((4, 4, 8, 512), BF16),
             pltpu.VMEM((3, 3, 3, 4, 32), BF16),
@@ -269,7 +269,7 @@
             pltpu.SemaphoreType.DMA((16,)),
         ],
         compiler_params=pltpu.CompilerParams(
-            collective_id=0, has_side_effects=True, vmem_limit_bytes=48 * 2**20
+            collective_id=0, has_side_effects=True
         ),
         cost_estimate=pl.CostEstimate(flops=2 * 10**9, bytes_accessed=3 * 10**6, transcendentals=0),
         name="layers",

time: 36.3 us -> 29.4 us (0.81)
  local copies, waits for them, and re-layouts: 6.49 us -> 0.63 us
  Pallas kernels: 29.5 us -> 28.6 us
    unnamed x13 -> x1, local copies, waits for them, and re-layouts: 6.49 us -> 0.63 us
    pallas_call x1, Pallas kernels: 29.5 us -> 28.6 us  [shards(): pl.pallas_call(functools.partial(body, depths, heights), out_shape=pltpu....]
where the time goes in v2:
time: 29.4 us; the launch traced here: 29.3 us
  Pallas kernels  28.6 us (97%)
  local copies, waits for them, and re-layouts  0.63 us (2%)
    pallas_call x1, Pallas kernels, shards(): pl.pallas_call(functools.partial(body, depths, heights), out_shape=pltpu....  28.6 us
    unnamed x1, local copies, waits for them, and re-layouts  0.63 us

profile of v2, /device:TPU:31, one launch (start us, length us, event | category | flops | bytes accessed | tf_op | source)
XLA Modules:
  0.0 29.3 jit_solution(8601536049309458409)
XLA Ops:
  0.0 28.6 %layers.1 = bf16[256,128]{1,0:T(8,128)(2,1)S(1)} custom-call(bf16[4,4,8,512]{3,2,1,0:T(8,128)(2,1)} %volume.1, bf16[3,3,3,4,32]{4,3,2,1,0:T(4,128)(2,1)} %first.1, bf16[3,3,96,64]{3,2,1,0:T(8,128)(2,1)} %bitcast.7, bf16[3,3,192,128]{3,2,1,0:T(8,128)(2,1)} %bitcast.6, bf16[512,512]{1,0:T(8,128)(2,1)} %constant.4.clone.phases, ...), custom_call_target="tpu_custom_call" | custom-call | flops 2000000000 | bytes 3000000 | tf_op jit(solution)/shard_map/layers/pallas_call | solution.py:242
  28.7 0.6 %copy.9 = bf16[128,1,2,128]{3,2,1,0:T(2,128)(2,1)} copy(bf16[128,1,2,128]{3,2,1,0:T(2,128)(2,1)S(1)} %bitcast.5) | data formatting | bytes 131072

commit v3 on v2

v3 whole, which is shorter than its diff:
```python
import functools

import jax
import jax.numpy as jnp
import numpy as np
from jax import lax
from jax.experimental import pallas as pl
from jax.experimental.pallas import tpu as pltpu
from jax.sharding import PartitionSpec as P

MESH = pl.DeviceIdType.MESH
BF16 = jnp.bfloat16
F32 = jnp.float32
SLOPE = 0.3
SIDES = [(a, b) for b in (-1, 1, 0) for a in (0, -1, 1) if (a, b) != (0, 0)]


def phase_matrix():
    cell = lax.broadcasted_iota(jnp.int32, (512, 512), 0)
    column = lax.broadcasted_iota(jnp.int32, (512, 512), 1)
    return jnp.where(cell == 4 * (column & 127) + (column >> 7), 1.0, 0.0).astype(BF16)


def first_placement():
    place = np.zeros((3, 3, 3, 4, 2, 2, 2, 2, 4, 4, 4, 4), np.float32)
    order = ((1, 2, 3, 0), (3, 0, 1, 2))
    for a, b, e, c, s, pd, ph, pw in np.ndindex(3, 3, 3, 4, 2, 2, 2, 2):
        place[a, b, e, c, s, pd, ph, pw, pd + a, ph + b, order[s].index(pw + e), c] = 1
    return np.pad(place.reshape(108, 4096), ((0, 20), (0, 0)))


def nt_dot(left, right):
    return lax.dot_general(left, right, (((1,), (1,)), ((), ())), preferred_element_type=F32)


def dot(left, right):
    return jnp.dot(left, right, preferred_element_type=F32)


def eye(size):
    rows = lax.broadcasted_iota(jnp.int32, (size, size), 0)
    columns = lax.broadcasted_iota(jnp.int32, (size, size), 1)
    return jnp.where(rows == columns, 1.0, 0.0).astype(BF16)


def before(value):
    lane = lax.broadcasted_iota(jnp.int32, value.shape, 1)
    return jnp.where(lane == 0, jnp.zeros_like(value), pltpu.roll(value, 1, 1))


def after(value):
    lane = lax.broadcasted_iota(jnp.int32, value.shape, 1)
    return jnp.where(lane == 127, jnp.zeros_like(value), pltpu.roll(value, 127, 1))


def leaky(value):
    return jnp.where(value > 0, value, SLOPE * value)


def span(shift, size, halo, received):
    if shift == 0:
        return pl.ds(halo, size)
    if received:
        return pl.ds(0, halo) if shift == 1 else pl.ds(halo + size, halo)
    return pl.ds(size, halo) if shift == 1 else pl.ds(halo, halo)


def body(
    depths, heights,
    volume, first, second, third, placement, out,
    x, k1, k2, k3, place, y, g, e0, e1, k1f, w1, f, w2, t, u, w3, acc, of,
    load_sem, send_sem, recv_sem,
):
    di, hi = lax.axis_index("depth"), lax.axis_index("height")

    def within(a, b):
        return (di + a >= 0) & (di + a < depths) & (hi + b >= 0) & (hi + b < heights)

    barrier = pltpu.get_barrier_semaphore()
    for a, b in SIDES:
        @pl.when(within(a, b))
        def _():
            pl.semaphore_signal(barrier, inc=1, device_id=(di + a, hi + b), device_id_type=MESH)

    loads = [
        pltpu.make_async_copy(source, target, load_sem.at[i])
        for i, (source, target) in enumerate(
            ((volume, x), (first, k1), (placement, place), (second, k2), (third, k3))
        )
    ]
    for load in loads:
        load.start()

    for a, b in SIDES:
        @pl.when(jnp.logical_not(within(-a, -b)))
        def _():
            d1, h1 = span(a, 4, 3, True), span(b, 8, 3, True)
            g[d1, h1] = jnp.zeros((d1.size, h1.size, 16, 128), BF16)
            d2, h2 = span(a, 1, 1, True), span(b, 2, 1, True)
            t[d2, h2] = jnp.zeros((d2.size, h2.size, 64, 128), BF16)

    phase = phase_matrix()
    loads[0].wait()
    spread = dot(x[...].reshape(128, 512), phase)
    for i in range(4):
        y[pl.ds(i * 128, 128), :] = spread[:, i * 128 : (i + 1) * 128]
    for d in range(4):
        for h in range(8):
            g[3 + d, 3 + h] = y[pl.ds(d * 8 + h, 16, stride=32), :].astype(BF16)

    count_d = 1 + (di > 0).astype(jnp.int32) + (di < depths - 1).astype(jnp.int32)
    count_h = 1 + (hi > 0).astype(jnp.int32) + (hi < heights - 1).astype(jnp.int32)
    pl.semaphore_wait(barrier, count_d * count_h - 1)

    halo = []
    for i, (a, b) in enumerate(SIDES):
        copy = pltpu.make_async_remote_copy(
            src_ref=g.at[span(a, 4, 3, False), span(b, 8, 3, False)],
            dst_ref=g.at[span(a, 4, 3, True), span(b, 8, 3, True)],
            send_sem=send_sem.at[i],
            recv_sem=recv_sem.at[i],
            device_id=(di + a, hi + b),
            device_id_type=MESH,
        )
        pl.when(within(a, b))(copy.start)
        halo.append(((a, b), copy))

    def arrive(shift):
        for (a, b), copy in halo:
            if b == shift:
                pl.when(within(-a, -b))(copy.wait_recv)

    def row_copy(r, a, b, index):
        return pltpu.make_async_remote_copy(
            src_ref=t.at[1, 1 + r],
            dst_ref=t.at[1 - a, 1 + r if b is None else 3 - 3 * r],
            send_sem=send_sem.at[8 + 5 * r + index],
            recv_sem=recv_sem.at[8 + 5 * r + index],
            device_id=(di + a, hi if b is None else hi + b),
            device_id_type=MESH,
        )

    def row_copies(r):
        b = 2 * r - 1
        side = [(a, b, row_copy(r, a, b, 2 + i)) for i, a in enumerate((0, -1, 1))]
        return side + [(a, 0, row_copy(r, a, None, i)) for i, a in enumerate((-1, 1))]

    for load in loads[1:]:
        load.wait()
    k1f[...] = jnp.zeros_like(k1f)
    for i, (a, b, e) in enumerate(np.ndindex(3, 3, 3)):
        k1f[pl.ds(4 * i, 4), :] = k1[a, b, e].astype(F32)
    flat = nt_dot(eye(32), k1f[...].astype(BF16)).astype(BF16)
    for s in range(2):
        for p in range(0, 8, 4):
            wide = dot(flat, place[:, pl.ds((s * 8 + p) * 256, 1024)]).astype(BF16)
            for q in range(4):
                w1[s, pl.ds((p + q) * 32, 32), :] = wide[:, q * 256 : (q + 1) * 256]

    unit = eye(64)
    blank = jnp.zeros((32, 64), BF16)
    for a in range(3):
        for b in range(3):
            taps = k2[a, b].reshape(96, 64)
            turned = nt_dot(unit, jnp.concatenate([taps, blank, blank, taps], 0)).astype(BF16)
            for ph in range(2):
                for pw in range(2):
                    w2[pl.ds(ph * 128 + pw * 64, 64), pl.ds((a * 4 + b + ph) * 128, 128)] = turned[
                        :, pw * 128 : (pw + 1) * 128
                    ]
        for ph, h in ((0, 3), (1, 0)):
            w2[pl.ds(ph * 128, 128), pl.ds((a * 4 + h) * 128, 128)] = jnp.zeros((128, 128), BF16)

    unit = eye(128)
    for i in range(9):
        rows = k3[i // 3, i % 3].reshape(192, 128)
        w3[i] = nt_dot(unit, rows).astype(BF16)

    def widen(d0, depth, h0, height):
        here = pl.ds(d0, depth), pl.ds(h0, height)
        value = g[here].reshape(depth * height * 16, 128)
        row = lax.broadcasted_iota(jnp.int32, value.shape, 0) & 15
        shape = (depth, height, 16, 128)
        e0[here] = jnp.where(row >= 12, before(value), value).reshape(shape)
        e1[here] = jnp.where(row < 4, after(value), value).reshape(shape)

    def first_layer(hp):
        for dp in range(4):
            deep = 2 * di + dp - 1
            deep_in = (deep >= 0) & (deep < 2 * depths)
            halves = []
            for s, e in enumerate((e0, e1)):
                parts = [
                    e[pl.ds(2 * dp, 4), pl.ds(2 * (hp + j), 4)].reshape(256, 128) for j in range(2)
                ]
                sums = dot(w1[s], jnp.concatenate(parts, 1))
                halves.append(leaky(jnp.max(sums.reshape(8, 32, 256), axis=0)))
            for j in range(2):
                tall = 4 * hi + hp + j - 1
                keep = jnp.where(deep_in & (tall >= 0) & (tall < 4 * heights), 1.0, 0.0)
                p0, p1 = ((half[:, j * 128 : (j + 1) * 128] * keep).astype(BF16) for half in halves)
                for i, part in enumerate((before(p1), p0, p1, after(p0))):
                    f[dp, hp + j, pl.ds(32 * i, 32), :] = part

    widen(3, 4, 3, 8)
    arrive(0)
    widen(0, 3, 3, 8)
    widen(7, 3, 3, 8)
    first_layer(2)

    turn = ((hi & 7) == 0).astype(jnp.int32)

    @pl.loop(0, 2)
    def _(k):
        r = k + turn * (1 - 2 * k)
        pl.when(r == 0)(lambda: arrive(1))
        pl.when(r == 1)(lambda: arrive(-1))
        widen(0, 10, 11 * r, 3)
        first_layer(4 * r)
        parts = [f[pl.ds(pd, 3), pl.ds(2 * r, 4)].reshape(1536, 128) for pd in range(2)]
        sums = dot(w2[...], jnp.concatenate(parts, 1))
        sums = jnp.max(sums.reshape(4, 64, 256), axis=0)
        t[1, 1 + r] = leaky(jnp.maximum(sums[:, 0:128], sums[:, 128:256])).astype(BF16)
        for a, b, copy in row_copies(r):
            pl.when(within(a, b))(copy.start)

    def spread_taps(d, h):
        value = t[d, h]
        u[d, h, pl.ds(0, 64), :] = before(value)
        u[d, h, pl.ds(64, 64), :] = value
        u[d, h, pl.ds(128, 64), :] = after(value)

    spread_taps(1, 1)
    spread_taps(1, 2)
    for r in range(2):
        for a, b, copy in row_copies(r)[3:]:
            pl.when(within(-a, 0))(copy.wait_recv)
    for d in (0, 2):
        for h in (1, 2):
            spread_taps(d, h)
    totals = [None, None]
    for d in range(3):
        both = dot(w3[3 * d + 1], jnp.concatenate([u[d, 1], u[d, 2]], 1))
        terms = both[:, 0:128] + dot(w3[3 * d + 2], u[d, 2]), both[:, 128:256] + dot(w3[3 * d], u[d, 1])
        totals = [term if total is None else total + term for total, term in zip(totals, terms)]
    for j in range(2):
        acc[j] = totals[j]

    @pl.loop(0, 2)
    def _(k):
        side = k + turn * (1 - 2 * k)
        for a, b, copy in row_copies(1 - side)[:3]:
            pl.when(within(-a, -b))(copy.wait_recv)
        total = acc[side]
        for d in range(3):
            spread_taps(d, 3 * side)
            total = total + dot(w3[3 * d + 2 * side], u[d, 3 * side])
        of[pl.ds(side, 128, stride=2), :] = leaky(total)

    out[...] = of[...].astype(BF16)
    for (a, b), copy in halo:
        pl.when(within(a, b))(copy.wait_send)
    for r in range(2):
        for a, b, copy in row_copies(r):
            pl.when(within(a, b))(copy.wait_send)


def shards(depths, heights, volume, first, second, third):
    placement = jnp.asarray(first_placement(), BF16)
    result = pl.pallas_call(
        functools.partial(body, depths, heights),
        out_shape=pltpu.VMEM((256, 128), BF16),
        in_specs=[pl.BlockSpec(memory_space=pltpu.HBM)] * 5,
        out_specs=pl.BlockSpec(memory_space=pltpu.VMEM),
        scratch_shapes=[
            pltpu.VMEM((4, 4, 8, 512), BF16),
            pltpu.VMEM((3, 3, 3, 4, 32), BF16),
            pltpu.VMEM((3, 3, 96, 64), BF16),
            pltpu.VMEM((3, 3, 192, 128), BF16),
            pltpu.VMEM((128, 4096), BF16),
            pltpu.VMEM((512, 128), F32),
            pltpu.VMEM((10, 14, 16, 128), BF16),
            pltpu.VMEM((10, 14, 16, 128), BF16),
            pltpu.VMEM((10, 14, 16, 128), BF16),
            pltpu.VMEM((128, 32), F32),
            pltpu.VMEM((2, 256, 256), BF16),
            pltpu.VMEM((4, 6, 128, 128), BF16),
            pltpu.VMEM((256, 1536), BF16),
            pltpu.VMEM((3, 4, 64, 128), BF16),
            pltpu.VMEM((3, 4, 192, 128), BF16),
            pltpu.VMEM((9, 128, 192), BF16),
            pltpu.VMEM((2, 128, 128), F32),
            pltpu.VMEM((256, 128), F32),
            pltpu.SemaphoreType.DMA((5,)),
            pltpu.SemaphoreType.DMA((18,)),
            pltpu.SemaphoreType.DMA((18,)),
        ],
        compiler_params=pltpu.CompilerParams(
            collective_id=0, has_side_effects=True
        ),
        cost_estimate=pl.CostEstimate(flops=2 * 10**9, bytes_accessed=3 * 10**6, transcendentals=0),
        name="layers",
    )(volume, first, second.reshape(3, 3, 96, 64), third.reshape(3, 3, 192, 128), placement)
    return result.reshape(128, 1, 2, 128)


def solution(mesh):
    in_specs = (P(None, "depth", "height", None), P(), P(), P())
    out_specs = P(None, "depth", "height", None)
    local = functools.partial(shards, mesh.shape["depth"], mesh.shape["height"])
    return jax.shard_map(local, mesh=mesh, in_specs=in_specs, out_specs=out_specs, check_vma=False)
```

time: 29.4 us -> 26.5 us (0.901)
  Pallas kernels: 28.6 us -> 25.8 us
    pallas_call x1, Pallas kernels: 28.6 us -> 25.8 us  [shards(): pl.pallas_call(functools.partial(body, depths, heights), out_shape=pltpu....]
where the time goes in v3:
time: 26.5 us; the launch traced here: 26.4 us
  Pallas kernels  25.8 us (97%)
  local copies, waits for them, and re-layouts  0.63 us (2%)
    pallas_call x1, Pallas kernels, shards(): pl.pallas_call(functools.partial(body, depths, heights), out_shape=pltpu....  25.8 us
    unnamed x1, local copies, waits for them, and re-layouts  0.63 us

profile of v3, /device:TPU:31, one launch (start us, length us, event | category | flops | bytes accessed | tf_op | source)
XLA Modules:
  0.0 26.4 jit_solution(661459807979400663)
XLA Ops:
  0.0 25.8 %layers.1 = bf16[256,128]{1,0:T(8,128)(2,1)S(1)} custom-call(bf16[4,4,8,512]{3,2,1,0:T(8,128)(2,1)} %volume.1, bf16[3,3,3,4,32]{4,3,2,1,0:T(4,128)(2,1)} %first.1, bf16[3,3,96,64]{3,2,1,0:T(8,128)(2,1)} %bitcast.7, bf16[3,3,192,128]{3,2,1,0:T(8,128)(2,1)} %bitcast.6, bf16[128,4096]{1,0:T(8,128)(2,1)} %constant.2.clone.placement), custom_call_target="tpu_custom_call" | custom-call | flops 2000000000 | bytes 3000000 | tf_op jit(solution)/shard_map/layers/pallas_call | solution.py:270
  25.8 0.6 %copy.8 = bf16[128,1,2,128]{3,2,1,0:T(2,128)(2,1)} copy(bf16[128,1,2,128]{3,2,1,0:T(2,128)(2,1)S(1)} %bitcast.5) | data formatting | bytes 131072

commit v4 on v3

--- a/solution.py
+++ b/solution.py
@@ -12,7 +12,8 @@
 BF16 = jnp.bfloat16
 F32 = jnp.float32
 SLOPE = 0.3
-SIDES = [(a, b) for b in (-1, 1, 0) for a in (0, -1, 1) if (a, b) != (0, 0)]
+RING = 8
+SIDES = [(a, b) for b in (1, -1, 0) for a in (0, -1, 1) if (a, b) != (0, 0)]
 
 
 def phase_matrix():
@@ -68,19 +69,13 @@
 def body(
     depths, heights,
     volume, first, second, third, placement, out,
-    x, k1, k2, k3, place, y, g, e0, e1, k1f, w1, f, w2, t, u, w3, acc, of,
-    load_sem, send_sem, recv_sem,
+    x, k1, k2, k3, place, y, g, e0, e1, k1f, w1, f, w2, half, t, u, w3, acc, of,
+    passed, load_sem, send_sem, recv_sem, door,
 ):
     di, hi = lax.axis_index("depth"), lax.axis_index("height")
 
     def within(a, b):
         return (di + a >= 0) & (di + a < depths) & (hi + b >= 0) & (hi + b < heights)
-
-    barrier = pltpu.get_barrier_semaphore()
-    for a, b in SIDES:
-        @pl.when(within(a, b))
-        def _():
-            pl.semaphore_signal(barrier, inc=1, device_id=(di + a, hi + b), device_id_type=MESH)
 
     loads = [
         pltpu.make_async_copy(source, target, load_sem.at[i])
@@ -88,7 +83,25 @@
             ((volume, x), (first, k1), (placement, place), (second, k2), (third, k3))
         )
     ]
-    for load in loads:
+    loads[0].start()
+
+    late = (lax.rem(hi, RING) == RING - 1) & (hi + 1 < heights)
+    source = (lax.rem(hi, RING) == 0) & (hi > 0)
+    relay = (lax.rem(hi, RING) == 0) & (hi + RING < heights)
+
+    barrier = pltpu.get_barrier_semaphore()
+
+    def greet(semaphore, a, b, condition):
+        @pl.when(condition & within(a, b))
+        def _():
+            pl.semaphore_signal(semaphore, inc=1, device_id=(di + a, hi + b), device_id_type=MESH)
+
+    for a, b in SIDES:
+        greet(barrier, a, b, jnp.logical_not(late) if b == 1 else True)
+    for a in (0, -1, 1):
+        greet(barrier, a, RING - 1, relay)
+    greet(barrier, 0, RING, relay)
+    for load in loads[1:]:
         load.start()
 
     for a, b in SIDES:
@@ -110,7 +123,22 @@
 
     count_d = 1 + (di > 0).astype(jnp.int32) + (di < depths - 1).astype(jnp.int32)
     count_h = 1 + (hi > 0).astype(jnp.int32) + (hi < heights - 1).astype(jnp.int32)
-    pl.semaphore_wait(barrier, count_d * count_h - 1)
+    more = jnp.where(late, count_d, 0) + jnp.where(source, 1 - count_d, 0)
+    pl.semaphore_wait(barrier, count_d * count_h - 1 + more)
+    for a in (0, -1, 1):
+        greet(door.at[2 - a], a, 1 - RING, late)
+    for a in (0, -1, 1):
+        greet(door.at[0], a, 1, late)
+
+    passing = pltpu.make_async_remote_copy(
+        src_ref=g.at[pl.ds(3, 4), pl.ds(3, 3)],
+        dst_ref=passed,
+        send_sem=send_sem.at[21],
+        recv_sem=recv_sem.at[18],
+        device_id=(di, hi - RING),
+        device_id_type=MESH,
+    )
+    pl.when(source)(passing.start)
 
     halo = []
     for i, (a, b) in enumerate(SIDES):
@@ -122,11 +150,25 @@
             device_id=(di + a, hi + b),
             device_id_type=MESH,
         )
-        pl.when(within(a, b))(copy.start)
-        halo.append(((a, b), copy))
+        direct = within(a, b) & jnp.logical_not(source) if b == -1 else within(a, b)
+        pl.when(direct)(copy.start)
+        halo.append(((a, b), copy, direct))
+
+    relayed = []
+    for i, a in enumerate((0, -1, 1)):
+        first_plane, planes = (max(a, 0), 4 - abs(a))
+        copy = pltpu.make_async_remote_copy(
+            src_ref=passed.at[pl.ds(first_plane, planes)],
+            dst_ref=g.at[span(a, 4, 3, True), span(-1, 8, 3, True)],
+            send_sem=send_sem.at[18 + i],
+            recv_sem=recv_sem.at[SIDES.index((a, -1))],
+            device_id=(di + a, hi + RING - 1),
+            device_id_type=MESH,
+        )
+        relayed.append((a, copy))
 
     def arrive(shift):
-        for (a, b), copy in halo:
+        for (a, b), copy, direct in halo:
             if b == shift:
                 pl.when(within(-a, -b))(copy.wait_recv)
 
@@ -140,10 +182,10 @@
             device_id_type=MESH,
         )
 
-    def row_copies(r):
-        b = 2 * r - 1
-        side = [(a, b, row_copy(r, a, b, 2 + i)) for i, a in enumerate((0, -1, 1))]
-        return side + [(a, 0, row_copy(r, a, None, i)) for i, a in enumerate((-1, 1))]
+    row_copies = []
+    for r in range(2):
+        side = [(a, 2 * r - 1, row_copy(r, a, 2 * r - 1, 2 + i)) for i, a in enumerate((0, -1, 1))]
+        row_copies.append(side + [(a, 0, row_copy(r, a, None, i)) for i, a in enumerate((-1, 1))])
 
     for load in loads[1:]:
         load.wait()
@@ -165,11 +207,12 @@
             turned = nt_dot(unit, jnp.concatenate([taps, blank, blank, taps], 0)).astype(BF16)
             for ph in range(2):
                 for pw in range(2):
-                    w2[pl.ds(ph * 128 + pw * 64, 64), pl.ds((a * 4 + b + ph) * 128, 128)] = turned[
+                    h = b + ph
+                    w2[2 * a + h // 2, pl.ds(ph * 128 + pw * 64, 64), pl.ds(h % 2 * 128, 128)] = turned[
                         :, pw * 128 : (pw + 1) * 128
                     ]
         for ph, h in ((0, 3), (1, 0)):
-            w2[pl.ds(ph * 128, 128), pl.ds((a * 4 + h) * 128, 128)] = jnp.zeros((128, 128), BF16)
+            w2[2 * a + h // 2, pl.ds(ph * 128, 128), pl.ds(h % 2 * 128, 128)] = jnp.zeros((128, 128), BF16)
 
     unit = eye(128)
     for i in range(9):
@@ -202,27 +245,52 @@
                 for i, part in enumerate((before(p1), p0, p1, after(p0))):
                     f[dp, hp + j, pl.ds(32 * i, 32), :] = part
 
+    def second_layer(hp, later):
+        total = None
+        for a in range(3):
+            parts = [f[pd + a, pl.ds(hp, 2)].reshape(256, 128) for pd in range(2)]
+            term = dot(w2[2 * a + later], jnp.concatenate(parts, 1))
+            total = term if total is None else total + term
+        return total
+
     widen(3, 4, 3, 8)
     arrive(0)
     widen(0, 3, 3, 8)
     widen(7, 3, 3, 8)
     first_layer(2)
-
-    turn = ((hi & 7) == 0).astype(jnp.int32)
-
-    @pl.loop(0, 2)
-    def _(k):
-        r = k + turn * (1 - 2 * k)
-        pl.when(r == 0)(lambda: arrive(1))
-        pl.when(r == 1)(lambda: arrive(-1))
+    for r in range(2):
+        half[r] = second_layer(2, 1 - r)
+
+    def finish_row(r):
+        arrive(1 - 2 * r)
         widen(0, 10, 11 * r, 3)
         first_layer(4 * r)
-        parts = [f[pl.ds(pd, 3), pl.ds(2 * r, 4)].reshape(1536, 128) for pd in range(2)]
-        sums = dot(w2[...], jnp.concatenate(parts, 1))
+        sums = second_layer(4 * r, r) + half[r]
         sums = jnp.max(sums.reshape(4, 64, 256), axis=0)
         t[1, 1 + r] = leaky(jnp.maximum(sums[:, 0:128], sums[:, 128:256])).astype(BF16)
-        for a, b, copy in row_copies(r):
+        if r == 0:
+            pl.when(source)(lambda: pl.semaphore_wait(door.at[0], count_d))
+        for a, b, copy in row_copies[r]:
             pl.when(within(a, b))(copy.start)
+
+    @pl.when(source | late)
+    def _():
+        finish_row(1)
+        finish_row(0)
+
+    @pl.when(jnp.logical_not(source | late))
+    def _():
+        finish_row(0)
+        finish_row(1)
+
+    @pl.when(relay)
+    def _():
+        passing.wait_recv()
+        for a, copy in relayed:
+            @pl.when(within(a, 0))
+            def _():
+                pl.semaphore_wait(door.at[2 + a], 1)
+                copy.start()
 
     def spread_taps(d, h):
         value = t[d, h]
@@ -233,7 +301,7 @@
     spread_taps(1, 1)
     spread_taps(1, 2)
     for r in range(2):
-        for a, b, copy in row_copies(r)[3:]:
+        for a, b, copy in row_copies[r][3:]:
             pl.when(within(-a, 0))(copy.wait_recv)
     for d in (0, 2):
         for h in (1, 2):
@@ -243,25 +311,24 @@
         both = dot(w3[3 * d + 1], jnp.concatenate([u[d, 1], u[d, 2]], 1))
         terms = both[:, 0:128] + dot(w3[3 * d + 2], u[d, 2]), both[:, 128:256] + dot(w3[3 * d], u[d, 1])
         totals = [term if total is None else total + term for total, term in zip(totals, terms)]
-    for j in range(2):
-        acc[j] = totals[j]
-
-    @pl.loop(0, 2)
-    def _(k):
-        side = k + turn * (1 - 2 * k)
-        for a, b, copy in row_copies(1 - side)[:3]:
+
+    for side in (1, 0):
+        for a, b, copy in row_copies[1 - side][:3]:
             pl.when(within(-a, -b))(copy.wait_recv)
-        total = acc[side]
+        total = totals[side]
         for d in range(3):
             spread_taps(d, 3 * side)
             total = total + dot(w3[3 * d + 2 * side], u[d, 3 * side])
         of[pl.ds(side, 128, stride=2), :] = leaky(total)
 
     out[...] = of[...].astype(BF16)
-    for (a, b), copy in halo:
-        pl.when(within(a, b))(copy.wait_send)
+    pl.when(source)(passing.wait_send)
+    for a, copy in relayed:
+        pl.when(relay & within(a, 0))(copy.wait_send)
+    for _, copy, direct in halo:
+        pl.when(direct)(copy.wait_send)
     for r in range(2):
-        for a, b, copy in row_copies(r):
+        for a, b, copy in row_copies[r]:
             pl.when(within(a, b))(copy.wait_send)
 
 
@@ -285,15 +352,18 @@
             pltpu.VMEM((128, 32), F32),
             pltpu.VMEM((2, 256, 256), BF16),
             pltpu.VMEM((4, 6, 128, 128), BF16),
-            pltpu.VMEM((256, 1536), BF16),
+            pltpu.VMEM((6, 256, 256), BF16),
+            pltpu.VMEM((2, 256, 256), F32),
             pltpu.VMEM((3, 4, 64, 128), BF16),
             pltpu.VMEM((3, 4, 192, 128), BF16),
             pltpu.VMEM((9, 128, 192), BF16),
             pltpu.VMEM((2, 128, 128), F32),
             pltpu.VMEM((256, 128), F32),
+            pltpu.VMEM((4, 3, 16, 128), BF16),
             pltpu.SemaphoreType.DMA((5,)),
-            pltpu.SemaphoreType.DMA((18,)),
-            pltpu.SemaphoreType.DMA((18,)),
+            pltpu.SemaphoreType.DMA((22,)),
+            pltpu.SemaphoreType.DMA((19,)),
+            pltpu.SemaphoreType.REGULAR((4,)),
         ],
         compiler_params=pltpu.CompilerParams(
             collective_id=0, has_side_effects=True

time: 26.5 us -> 25.7 us (0.970)
  the two profiles are of different devices: /device:TPU:31 before, /device:TPU:7 now
where the time goes in v4:
time: 25.7 us; the launch traced here: 25.5 us
  Pallas kernels  24.9 us (97%)
  local copies, waits for them, and re-layouts  0.63 us (2%)
    pallas_call x1, Pallas kernels, shards(): pl.pallas_call(functools.partial(body, depths, heights), out_shape=pltpu....  24.9 us
    unnamed x1, local copies, waits for them, and re-layouts  0.63 us

profile of v4, /device:TPU:7, one launch (start us, length us, event | category | flops | bytes accessed | tf_op | source)
XLA Modules:
  0.0 25.5 jit_solution(12618552475381123754)
XLA Ops:
  0.0 24.9 %layers.1 = bf16[256,128]{1,0:T(8,128)(2,1)S(1)} custom-call(bf16[4,4,8,512]{3,2,1,0:T(8,128)(2,1)} %volume.1, bf16[3,3,3,4,32]{4,3,2,1,0:T(4,128)(2,1)} %first.1, bf16[3,3,96,64]{3,2,1,0:T(8,128)(2,1)} %bitcast.7, bf16[3,3,192,128]{3,2,1,0:T(8,128)(2,1)} %bitcast.6, bf16[128,4096]{1,0:T(8,128)(2,1)} %constant.2.clone.placement), custom_call_target="tpu_custom_call" | custom-call | flops 2000000000 | bytes 3000000 | tf_op jit(solution)/shard_map/layers/pallas_call | solution.py:337
  24.9 0.6 %copy.8 = bf16[128,1,2,128]{3,2,1,0:T(2,128)(2,1)} copy(bf16[128,1,2,128]{3,2,1,0:T(2,128)(2,1)S(1)} %bitcast.5) | data formatting | bytes 131072

commit v5 on v4

--- a/solution.py
+++ b/solution.py
@@ -13,7 +13,7 @@
 F32 = jnp.float32
 SLOPE = 0.3
 RING = 8
-SIDES = [(a, b) for b in (1, -1, 0) for a in (0, -1, 1) if (a, b) != (0, 0)]
+SIDES = [(a, b) for b in (0, 1, -1) for a in (0, -1, 1) if (a, b) != (0, 0)]
 
 
 def phase_matrix():
@@ -70,7 +70,7 @@
     depths, heights,
     volume, first, second, third, placement, out,
     x, k1, k2, k3, place, y, g, e0, e1, k1f, w1, f, w2, half, t, u, w3, acc, of,
-    passed, load_sem, send_sem, recv_sem, door,
+    passed, load_sem, send_sem, recv_sem, door, go,
 ):
     di, hi = lax.axis_index("depth"), lax.axis_index("height")
 
@@ -85,9 +85,9 @@
     ]
     loads[0].start()
 
-    late = (lax.rem(hi, RING) == RING - 1) & (hi + 1 < heights)
-    source = (lax.rem(hi, RING) == 0) & (hi > 0)
-    relay = (lax.rem(hi, RING) == 0) & (hi + RING < heights)
+    rings = heights == 2 * RING
+    late, source = (hi == RING - 1) & rings, (hi == RING) & rings
+    relay, herald = (hi == 0) & rings, (hi == 1) & rings
 
     barrier = pltpu.get_barrier_semaphore()
 
@@ -97,9 +97,9 @@
             pl.semaphore_signal(semaphore, inc=1, device_id=(di + a, hi + b), device_id_type=MESH)
 
     for a, b in SIDES:
-        greet(barrier, a, b, jnp.logical_not(late) if b == 1 else True)
+        greet(barrier, a, b, jnp.logical_not({1: late, 0: relay, -1: herald}[b]))
     for a in (0, -1, 1):
-        greet(barrier, a, RING - 1, relay)
+        greet(barrier, a, 1 - RING, late)
     greet(barrier, 0, RING, relay)
     for load in loads[1:]:
         load.start()
@@ -123,12 +123,12 @@
 
     count_d = 1 + (di > 0).astype(jnp.int32) + (di < depths - 1).astype(jnp.int32)
     count_h = 1 + (hi > 0).astype(jnp.int32) + (hi < heights - 1).astype(jnp.int32)
-    more = jnp.where(late, count_d, 0) + jnp.where(source, 1 - count_d, 0)
-    pl.semaphore_wait(barrier, count_d * count_h - 1 + more)
+    around = count_d * count_h - 1 + jnp.where(source, 1 - count_d, 0)
+    pl.when(jnp.logical_not(relay))(lambda: pl.semaphore_wait(barrier, around))
+    greet(go, 0, -1, herald)
     for a in (0, -1, 1):
-        greet(door.at[2 - a], a, 1 - RING, late)
-    for a in (0, -1, 1):
-        greet(door.at[0], a, 1, late)
+        greet(door, a, 1, late)
+    pl.when(relay)(lambda: pl.semaphore_wait(go, 1))
 
     passing = pltpu.make_async_remote_copy(
         src_ref=g.at[pl.ds(3, 4), pl.ds(3, 3)],
@@ -139,6 +139,19 @@
         device_id_type=MESH,
     )
     pl.when(source)(passing.start)
+
+    relayed = []
+    for i, a in enumerate((0, -1, 1)):
+        first_plane, planes = (max(a, 0), 4 - abs(a))
+        copy = pltpu.make_async_remote_copy(
+            src_ref=passed.at[pl.ds(first_plane, planes)],
+            dst_ref=g.at[span(a, 4, 3, True), span(-1, 8, 3, True)],
+            send_sem=send_sem.at[18 + i],
+            recv_sem=recv_sem.at[SIDES.index((a, -1))],
+            device_id=(di + a, hi + RING - 1),
+            device_id_type=MESH,
+        )
+        relayed.append((a, copy))
 
     halo = []
     for i, (a, b) in enumerate(SIDES):
@@ -153,19 +166,6 @@
         direct = within(a, b) & jnp.logical_not(source) if b == -1 else within(a, b)
         pl.when(direct)(copy.start)
         halo.append(((a, b), copy, direct))
-
-    relayed = []
-    for i, a in enumerate((0, -1, 1)):
-        first_plane, planes = (max(a, 0), 4 - abs(a))
-        copy = pltpu.make_async_remote_copy(
-            src_ref=passed.at[pl.ds(first_plane, planes)],
-            dst_ref=g.at[span(a, 4, 3, True), span(-1, 8, 3, True)],
-            send_sem=send_sem.at[18 + i],
-            recv_sem=recv_sem.at[SIDES.index((a, -1))],
-            device_id=(di + a, hi + RING - 1),
-            device_id_type=MESH,
-        )
-        relayed.append((a, copy))
 
     def arrive(shift):
         for (a, b), copy, direct in halo:
@@ -253,6 +253,13 @@
             total = term if total is None else total + term
         return total
 
+    @pl.when(relay)
+    def _():
+        pl.semaphore_wait(barrier, count_d)
+        passing.wait_recv()
+        for a, copy in relayed:
+            pl.when(within(a, 0))(copy.start)
+
     widen(3, 4, 3, 8)
     arrive(0)
     widen(0, 3, 3, 8)
@@ -269,7 +276,7 @@
         sums = jnp.max(sums.reshape(4, 64, 256), axis=0)
         t[1, 1 + r] = leaky(jnp.maximum(sums[:, 0:128], sums[:, 128:256])).astype(BF16)
         if r == 0:
-            pl.when(source)(lambda: pl.semaphore_wait(door.at[0], count_d))
+            pl.when(source)(lambda: pl.semaphore_wait(door, count_d))
         for a, b, copy in row_copies[r]:
             pl.when(within(a, b))(copy.start)
 
@@ -282,15 +289,6 @@
     def _():
         finish_row(0)
         finish_row(1)
-
-    @pl.when(relay)
-    def _():
-        passing.wait_recv()
-        for a, copy in relayed:
-            @pl.when(within(a, 0))
-            def _():
-                pl.semaphore_wait(door.at[2 + a], 1)
-                copy.start()
 
     def spread_taps(d, h):
         value = t[d, h]
@@ -363,7 +361,8 @@
             pltpu.SemaphoreType.DMA((5,)),
             pltpu.SemaphoreType.DMA((22,)),
             pltpu.SemaphoreType.DMA((19,)),
-            pltpu.SemaphoreType.REGULAR((4,)),
+            pltpu.SemaphoreType.REGULAR,
+            pltpu.SemaphoreType.REGULAR,
         ],
         compiler_params=pltpu.CompilerParams(
             collective_id=0, has_side_effects=True

time: 25.7 us -> 23.9 us (0.930)
  the two profiles are of different devices: /device:TPU:7 before, /device:TPU:31 now
where the time goes in v5:
time: 23.9 us; the launch traced here: 23.7 us
  Pallas kernels  23.1 us (97%)
  local copies, waits for them, and re-layouts  0.63 us (3%)
    pallas_call x1, Pallas kernels, shards(): pl.pallas_call(functools.partial(body, depths, heights), out_shape=pltpu....  23.1 us
    unnamed x1, local copies, waits for them, and re-layouts  0.63 us

profile of v5, /device:TPU:31, one launch (start us, length us, event | category | flops | bytes accessed | tf_op | source)
XLA Modules:
  0.0 23.7 jit_solution(1352064576634067144)
XLA Ops:
  0.0 23.1 %layers.1 = bf16[256,128]{1,0:T(8,128)(2,1)S(1)} custom-call(bf16[4,4,8,512]{3,2,1,0:T(8,128)(2,1)} %volume.1, bf16[3,3,3,4,32]{4,3,2,1,0:T(4,128)(2,1)} %first.1, bf16[3,3,96,64]{3,2,1,0:T(8,128)(2,1)} %bitcast.7, bf16[3,3,192,128]{3,2,1,0:T(8,128)(2,1)} %bitcast.6, bf16[128,4096]{1,0:T(8,128)(2,1)} %constant.2.clone.placement), custom_call_target="tpu_custom_call" | custom-call | flops 2000000000 | bytes 3000000 | tf_op jit(solution)/shard_map/layers/pallas_call | solution.py:335
  23.1 0.6 %copy.8 = bf16[128,1,2,128]{3,2,1,0:T(2,128)(2,1)} copy(bf16[128,1,2,128]{3,2,1,0:T(2,128)(2,1)S(1)} %bitcast.5) | data formatting | bytes 131072

commit v6 on v5

--- a/solution.py
+++ b/solution.py
@@ -69,8 +69,8 @@
 def body(
     depths, heights,
     volume, first, second, third, placement, out,
-    x, k1, k2, k3, place, y, g, e0, e1, k1f, w1, f, w2, half, t, u, w3, acc, of,
-    passed, load_sem, send_sem, recv_sem, door, go,
+    x, k1, k2, k3, place, y, g, e0, e1, k1f, w1, f, w2, t, u, w3, of,
+    passed, load_sem, send_sem, recv_sem, door, go, ready,
 ):
     di, hi = lax.axis_index("depth"), lax.axis_index("height")
 
@@ -96,24 +96,14 @@
         def _():
             pl.semaphore_signal(semaphore, inc=1, device_id=(di + a, hi + b), device_id_type=MESH)
 
+    greet(barrier, 0, 1 - RING, late)
     for a, b in SIDES:
         greet(barrier, a, b, jnp.logical_not({1: late, 0: relay, -1: herald}[b]))
-    for a in (0, -1, 1):
-        greet(barrier, a, 1 - RING, late)
     greet(barrier, 0, RING, relay)
+    phase = phase_matrix()
+    loads[0].wait()
     for load in loads[1:]:
         load.start()
-
-    for a, b in SIDES:
-        @pl.when(jnp.logical_not(within(-a, -b)))
-        def _():
-            d1, h1 = span(a, 4, 3, True), span(b, 8, 3, True)
-            g[d1, h1] = jnp.zeros((d1.size, h1.size, 16, 128), BF16)
-            d2, h2 = span(a, 1, 1, True), span(b, 2, 1, True)
-            t[d2, h2] = jnp.zeros((d2.size, h2.size, 64, 128), BF16)
-
-    phase = phase_matrix()
-    loads[0].wait()
     spread = dot(x[...].reshape(128, 512), phase)
     for i in range(4):
         y[pl.ds(i * 128, 128), :] = spread[:, i * 128 : (i + 1) * 128]
@@ -126,32 +116,47 @@
     around = count_d * count_h - 1 + jnp.where(source, 1 - count_d, 0)
     pl.when(jnp.logical_not(relay))(lambda: pl.semaphore_wait(barrier, around))
     greet(go, 0, -1, herald)
+    for a in (-1, 1):
+        greet(ready.at[(1 - a) // 2], a, 0, source)
     for a in (0, -1, 1):
         greet(door, a, 1, late)
     pl.when(relay)(lambda: pl.semaphore_wait(go, 1))
 
-    passing = pltpu.make_async_remote_copy(
-        src_ref=g.at[pl.ds(3, 4), pl.ds(3, 3)],
-        dst_ref=passed,
-        send_sem=send_sem.at[21],
-        recv_sem=recv_sem.at[18],
-        device_id=(di, hi - RING),
-        device_id_type=MESH,
-    )
-    pl.when(source)(passing.start)
-
-    relayed = []
+    passing, relayed = [], []
     for i, a in enumerate((0, -1, 1)):
-        first_plane, planes = (max(a, 0), 4 - abs(a))
         copy = pltpu.make_async_remote_copy(
-            src_ref=passed.at[pl.ds(first_plane, planes)],
-            dst_ref=g.at[span(a, 4, 3, True), span(-1, 8, 3, True)],
+            src_ref=g.at[span(a, 4, 3, False), pl.ds(3, 3)],
+            dst_ref=passed.at[span(a, 4, 3, True)],
             send_sem=send_sem.at[18 + i],
+            recv_sem=recv_sem.at[18 + i],
+            device_id=(di + a, hi - RING),
+            device_id_type=MESH,
+        )
+        passing.append((a, copy))
+        copy = pltpu.make_async_remote_copy(
+            src_ref=passed.at[span(a, 4, 3, True)],
+            dst_ref=g.at[span(a, 4, 3, True), pl.ds(11, 3)],
+            send_sem=send_sem.at[21 + i],
             recv_sem=recv_sem.at[SIDES.index((a, -1))],
-            device_id=(di + a, hi + RING - 1),
+            device_id=(di, hi + RING - 1),
             device_id_type=MESH,
         )
         relayed.append((a, copy))
+
+    pl.when(source)(passing[0][1].start)
+
+    mate = {1: lax.rem(di, 2) == 0, -1: lax.rem(di, 2) == 1}
+    shared = []
+    for i, a in enumerate((-1, 1)):
+        copy = pltpu.make_async_remote_copy(
+            src_ref=g.at[span(a, 4, 3, False), pl.ds(0, 3)],
+            dst_ref=g.at[span(a, 4, 3, True), pl.ds(0, 3)],
+            send_sem=send_sem.at[24 + i],
+            recv_sem=recv_sem.at[SIDES.index((a, 1))],
+            device_id=(di + a, hi),
+            device_id_type=MESH,
+        )
+        shared.append((source & mate[a], copy))
 
     halo = []
     for i, (a, b) in enumerate(SIDES):
@@ -163,14 +168,27 @@
             device_id=(di + a, hi + b),
             device_id_type=MESH,
         )
-        direct = within(a, b) & jnp.logical_not(source) if b == -1 else within(a, b)
+        direct = within(a, b)
+        if b == -1:
+            direct &= jnp.logical_not(source)
+        if b == 1 and a != 0:
+            direct &= jnp.logical_not(late & mate[a])
         pl.when(direct)(copy.start)
         halo.append(((a, b), copy, direct))
+
+    for a, copy in passing[1:]:
+        @pl.when(source & within(a, 0))
+        def _():
+            pl.semaphore_wait(ready.at[(1 + a) // 2], 1)
+            copy.start()
 
     def arrive(shift):
         for (a, b), copy, direct in halo:
             if b == shift:
                 pl.when(within(-a, -b))(copy.wait_recv)
+                if (a, b) == (0, 1):
+                    for condition, share in shared:
+                        pl.when(condition)(share.start)
 
     def row_copy(r, a, b, index):
         return pltpu.make_async_remote_copy(
@@ -186,6 +204,14 @@
     for r in range(2):
         side = [(a, 2 * r - 1, row_copy(r, a, 2 * r - 1, 2 + i)) for i, a in enumerate((0, -1, 1))]
         row_copies.append(side + [(a, 0, row_copy(r, a, None, i)) for i, a in enumerate((-1, 1))])
+
+    for a, b in SIDES:
+        @pl.when(jnp.logical_not(within(-a, -b)))
+        def _():
+            d1, h1 = span(a, 4, 3, True), span(b, 8, 3, True)
+            g[d1, h1] = jnp.zeros((d1.size, h1.size, 16, 128), BF16)
+            d2, h2 = span(a, 1, 1, True), span(b, 2, 1, True)
+            t[d2, h2] = jnp.zeros((d2.size, h2.size, 64, 128), BF16)
 
     for load in loads[1:]:
         load.wait()
@@ -255,24 +281,25 @@
 
     @pl.when(relay)
     def _():
-        pl.semaphore_wait(barrier, count_d)
-        passing.wait_recv()
-        for a, copy in relayed:
-            pl.when(within(a, 0))(copy.start)
+        pl.semaphore_wait(barrier, 1)
+        for (a, arriving), (_, leaving) in zip(passing, relayed):
+            @pl.when(within(-a, 0))
+            def _():
+                arriving.wait_recv()
+                leaving.start()
 
     widen(3, 4, 3, 8)
     arrive(0)
     widen(0, 3, 3, 8)
     widen(7, 3, 3, 8)
     first_layer(2)
-    for r in range(2):
-        half[r] = second_layer(2, 1 - r)
 
     def finish_row(r):
+        half = second_layer(2, 1 - r)
         arrive(1 - 2 * r)
         widen(0, 10, 11 * r, 3)
         first_layer(4 * r)
-        sums = second_layer(4 * r, r) + half[r]
+        sums = second_layer(4 * r, r) + half
         sums = jnp.max(sums.reshape(4, 64, 256), axis=0)
         t[1, 1 + r] = leaky(jnp.maximum(sums[:, 0:128], sums[:, 128:256])).astype(BF16)
         if r == 0:
@@ -296,35 +323,43 @@
         u[d, h, pl.ds(64, 64), :] = value
         u[d, h, pl.ds(128, 64), :] = after(value)
 
-    spread_taps(1, 1)
-    spread_taps(1, 2)
-    for r in range(2):
-        for a, b, copy in row_copies[r][3:]:
-            pl.when(within(-a, 0))(copy.wait_recv)
-    for d in (0, 2):
-        for h in (1, 2):
+    def add_row(h, depths_here):
+        for d in depths_here:
             spread_taps(d, h)
+            places = [j for j in range(2) if 0 <= h - j <= 2]
+            terms = dot(jnp.concatenate([w3[3 * d + h - j] for j in places], 0), u[d, h])
+            for i, j in enumerate(places):
+                term = terms[i * 128 : (i + 1) * 128]
+                totals[j] = term if totals[j] is None else totals[j] + term
+
+    def rows_arrive(r, side):
+        for a, b, copy in row_copies[r]:
+            if (b != 0) == side:
+                pl.when(within(-a, -b))(copy.wait_recv)
+
     totals = [None, None]
-    for d in range(3):
-        both = dot(w3[3 * d + 1], jnp.concatenate([u[d, 1], u[d, 2]], 1))
-        terms = both[:, 0:128] + dot(w3[3 * d + 2], u[d, 2]), both[:, 128:256] + dot(w3[3 * d], u[d, 1])
-        totals = [term if total is None else total + term for total, term in zip(totals, terms)]
-
-    for side in (1, 0):
-        for a, b, copy in row_copies[1 - side][:3]:
-            pl.when(within(-a, -b))(copy.wait_recv)
-        total = totals[side]
-        for d in range(3):
-            spread_taps(d, 3 * side)
-            total = total + dot(w3[3 * d + 2 * side], u[d, 3 * side])
-        of[pl.ds(side, 128, stride=2), :] = leaky(total)
-
-    out[...] = of[...].astype(BF16)
-    pl.when(source)(passing.wait_send)
+    add_row(1, (1,))
+    add_row(2, (1,))
+    for condition, copy in shared:
+        pl.when(condition)(copy.wait_send)
+    for a, copy in passing:
+        pl.when(source & within(a, 0))(copy.wait_send)
     for a, copy in relayed:
-        pl.when(relay & within(a, 0))(copy.wait_send)
+        pl.when(relay & within(-a, 0))(copy.wait_send)
     for _, copy, direct in halo:
         pl.when(direct)(copy.wait_send)
+    rows_arrive(1, False)
+    add_row(2, (0, 2))
+    rows_arrive(0, True)
+    add_row(3, (0, 1, 2))
+    rows_arrive(0, False)
+    add_row(1, (0, 2))
+    of[pl.ds(1, 128, stride=2), :] = leaky(totals[1])
+    rows_arrive(1, True)
+    add_row(0, (0, 1, 2))
+    of[pl.ds(0, 128, stride=2), :] = leaky(totals[0])
+
+    out[...] = of[...].astype(BF16)
     for r in range(2):
         for a, b, copy in row_copies[r]:
             pl.when(within(a, b))(copy.wait_send)
@@ -351,18 +386,17 @@
             pltpu.VMEM((2, 256, 256), BF16),
             pltpu.VMEM((4, 6, 128, 128), BF16),
             pltpu.VMEM((6, 256, 256), BF16),
-            pltpu.VMEM((2, 256, 256), F32),
             pltpu.VMEM((3, 4, 64, 128), BF16),
             pltpu.VMEM((3, 4, 192, 128), BF16),
             pltpu.VMEM((9, 128, 192), BF16),
-            pltpu.VMEM((2, 128, 128), F32),
             pltpu.VMEM((256, 128), F32),
-            pltpu.VMEM((4, 3, 16, 128), BF16),
+            pltpu.VMEM((10, 3, 16, 128), BF16),
             pltpu.SemaphoreType.DMA((5,)),
-            pltpu.SemaphoreType.DMA((22,)),
-            pltpu.SemaphoreType.DMA((19,)),
+            pltpu.SemaphoreType.DMA((26,)),
+            pltpu.SemaphoreType.DMA((21,)),
             pltpu.SemaphoreType.REGULAR,
             pltpu.SemaphoreType.REGULAR,
+            pltpu.SemaphoreType.REGULAR((2,)),
         ],
         compiler_params=pltpu.CompilerParams(
             collective_id=0, has_side_effects=True

time: 23.9 us -> 23.3 us (0.975)
  Pallas kernels: 23.1 us -> 22.6 us
    pallas_call x1, Pallas kernels: 23.1 us -> 22.6 us  [shards(): pl.pallas_call(functools.partial(body, depths, heights), out_shape=pltpu....]
where the time goes in v6:
time: 23.3 us; the launch traced here: 23.2 us
  Pallas kernels  22.6 us (97%)
  local copies, waits for them, and re-layouts  0.63 us (3%)
    pallas_call x1, Pallas kernels, shards(): pl.pallas_call(functools.partial(body, depths, heights), out_shape=pltpu....  22.6 us
    unnamed x1, local copies, waits for them, and re-layouts  0.63 us

profile of v6, /device:TPU:31, one launch (start us, length us, event | category | flops | bytes accessed | tf_op | source)
XLA Modules:
  0.0 23.2 jit_solution(11459526249835334429)
XLA Ops:
  0.0 22.6 %layers.1 = bf16[256,128]{1,0:T(8,128)(2,1)S(1)} custom-call(bf16[4,4,8,512]{3,2,1,0:T(8,128)(2,1)} %volume.1, bf16[3,3,3,4,32]{4,3,2,1,0:T(4,128)(2,1)} %first.1, bf16[3,3,96,64]{3,2,1,0:T(8,128)(2,1)} %bitcast.7, bf16[3,3,192,128]{3,2,1,0:T(8,128)(2,1)} %bitcast.6, bf16[128,4096]{1,0:T(8,128)(2,1)} %constant.2.clone.placement), custom_call_target="tpu_custom_call" | custom-call | flops 2000000000 | bytes 3000000 | tf_op jit(solution)/shard_map/layers/pallas_call | solution.py:370
  22.6 0.6 %copy.8 = bf16[128,1,2,128]{3,2,1,0:T(2,128)(2,1)} copy(bf16[128,1,2,128]{3,2,1,0:T(2,128)(2,1)S(1)} %bitcast.5) | data formatting | bytes 131072

commit v7 on v6

--- a/solution.py
+++ b/solution.py
@@ -69,7 +69,7 @@
 def body(
     depths, heights,
     volume, first, second, third, placement, out,
-    x, k1, k2, k3, place, y, g, e0, e1, k1f, w1, f, w2, t, u, w3, of,
+    x, k1, k2, k3, place, y, g, e0, e1, k1f, w1, f, w2, t, w3, of,
     passed, load_sem, send_sem, recv_sem, door, go, ready,
 ):
     di, hi = lax.axis_index("depth"), lax.axis_index("height")
@@ -319,15 +319,12 @@
 
     def spread_taps(d, h):
         value = t[d, h]
-        u[d, h, pl.ds(0, 64), :] = before(value)
-        u[d, h, pl.ds(64, 64), :] = value
-        u[d, h, pl.ds(128, 64), :] = after(value)
+        return jnp.concatenate([before(value), value, after(value)], 0)
 
     def add_row(h, depths_here):
         for d in depths_here:
-            spread_taps(d, h)
             places = [j for j in range(2) if 0 <= h - j <= 2]
-            terms = dot(jnp.concatenate([w3[3 * d + h - j] for j in places], 0), u[d, h])
+            terms = dot(jnp.concatenate([w3[3 * d + h - j] for j in places], 0), spread_taps(d, h))
             for i, j in enumerate(places):
                 term = terms[i * 128 : (i + 1) * 128]
                 totals[j] = term if totals[j] is None else totals[j] + term
@@ -355,14 +352,15 @@
     rows_arrive(0, False)
     add_row(1, (0, 2))
     of[pl.ds(1, 128, stride=2), :] = leaky(totals[1])
+    for a, b, copy in row_copies[1]:
+        pl.when(within(a, b))(copy.wait_send)
     rows_arrive(1, True)
     add_row(0, (0, 1, 2))
     of[pl.ds(0, 128, stride=2), :] = leaky(totals[0])
 
     out[...] = of[...].astype(BF16)
-    for r in range(2):
-        for a, b, copy in row_copies[r]:
-            pl.when(within(a, b))(copy.wait_send)
+    for a, b, copy in row_copies[0]:
+        pl.when(within(a, b))(copy.wait_send)
 
 
 def shards(depths, heights, volume, first, second, third):
@@ -387,7 +385,6 @@
             pltpu.VMEM((4, 6, 128, 128), BF16),
             pltpu.VMEM((6, 256, 256), BF16),
             pltpu.VMEM((3, 4, 64, 128), BF16),
-            pltpu.VMEM((3, 4, 192, 128), BF16),
             pltpu.VMEM((9, 128, 192), BF16),
             pltpu.VMEM((256, 128), F32),
             pltpu.VMEM((10, 3, 16, 128), BF16),

time: 23.3 us -> 23.3 us (level)
  no operation moved by 1% of the time
where the time goes in v7:
time: 23.3 us; the launch traced here: 23.2 us
  Pallas kernels  22.5 us (97%)
  local copies, waits for them, and re-layouts  0.63 us (3%)
    pallas_call x1, Pallas kernels, shards(): pl.pallas_call(functools.partial(body, depths, heights), out_shape=pltpu....  22.5 us
    unnamed x1, local copies, waits for them, and re-layouts  0.63 us

profile of v7, /device:TPU:31, one launch (start us, length us, event | category | flops | bytes accessed | tf_op | source)
XLA Modules:
  0.0 23.2 jit_solution(18377003588306641984)
XLA Ops:
  0.0 22.5 %layers.1 = bf16[256,128]{1,0:T(8,128)(2,1)S(1)} custom-call(bf16[4,4,8,512]{3,2,1,0:T(8,128)(2,1)} %volume.1, bf16[3,3,3,4,32]{4,3,2,1,0:T(4,128)(2,1)} %first.1, bf16[3,3,96,64]{3,2,1,0:T(8,128)(2,1)} %bitcast.7, bf16[3,3,192,128]{3,2,1,0:T(8,128)(2,1)} %bitcast.6, bf16[128,4096]{1,0:T(8,128)(2,1)} %constant.2.clone.placement), custom_call_target="tpu_custom_call" | custom-call | flops 2000000000 | bytes 3000000 | tf_op jit(solution)/shard_map/layers/pallas_call | solution.py:368
  22.5 0.6 %copy.8 = bf16[128,1,2,128]{3,2,1,0:T(2,128)(2,1)} copy(bf16[128,1,2,128]{3,2,1,0:T(2,128)(2,1)S(1)} %bitcast.5) | data formatting | bytes 131072

commit v8 on v7

--- a/solution.py
+++ b/solution.py
@@ -83,7 +83,6 @@
             ((volume, x), (first, k1), (placement, place), (second, k2), (third, k3))
         )
     ]
-    loads[0].start()
 
     rings = heights == 2 * RING
     late, source = (hi == RING - 1) & rings, (hi == RING) & rings
@@ -100,6 +99,8 @@
     for a, b in SIDES:
         greet(barrier, a, b, jnp.logical_not({1: late, 0: relay, -1: herald}[b]))
     greet(barrier, 0, RING, relay)
+    loads[0].start()
+
     phase = phase_matrix()
     loads[0].wait()
     for load in loads[1:]:

time: 23.3 us -> 23.3 us (level)
  no operation moved by 1% of the time
where the time goes in v8:
time: 23.3 us; the launch traced here: 23.2 us
  Pallas kernels  22.5 us (97%)
  local copies, waits for them, and re-layouts  0.63 us (3%)
    pallas_call x1, Pallas kernels, shards(): pl.pallas_call(functools.partial(body, depths, heights), out_shape=pltpu....  22.5 us
    unnamed x1, local copies, waits for them, and re-layouts  0.63 us

profile of v8, /device:TPU:31, one launch (start us, length us, event | category | flops | bytes accessed | tf_op | source)
XLA Modules:
  0.0 23.2 jit_solution(10360507570264641443)
XLA Ops:
  0.0 22.5 %layers.1 = bf16[256,128]{1,0:T(8,128)(2,1)S(1)} custom-call(bf16[4,4,8,512]{3,2,1,0:T(8,128)(2,1)} %volume.1, bf16[3,3,3,4,32]{4,3,2,1,0:T(4,128)(2,1)} %first.1, bf16[3,3,96,64]{3,2,1,0:T(8,128)(2,1)} %bitcast.7, bf16[3,3,192,128]{3,2,1,0:T(8,128)(2,1)} %bitcast.6, bf16[128,4096]{1,0:T(8,128)(2,1)} %constant.2.clone.placement), custom_call_target="tpu_custom_call" | custom-call | flops 2000000000 | bytes 3000000 | tf_op jit(solution)/shard_map/layers/pallas_call | solution.py:369
  22.5 0.6 %copy.8 = bf16[128,1,2,128]{3,2,1,0:T(2,128)(2,1)} copy(bf16[128,1,2,128]{3,2,1,0:T(2,128)(2,1)S(1)} %bitcast.5) | data formatting | bytes 131072
